TPU v7x, 32 devices: a whole 2x2x4 slice. The times are simulated.
32 devices in a mesh: post: 16 (over z, x, core), rep: 2 (over y).
Axes of the slice: x: 2, y: 2, z: 4, core: 2. Of those that a mesh axis runs over, the one named last changes fastest.
Arguments:
- split_vectors: bfloat16 [512, 192, 1024], P('post', None, 'rep'), may hold values from -6 to 6
- split_labels: int32 [512, 192], P('post'), may hold values from 0 to 1, as said below
- split_lengths: int32 [512], P('post'), may hold values from 144 to 192
- new_owners: int32 [512, 2], P('post'), may hold values from 0 to 15, all different within a row; in each aligned block of 32 rows (0 to 31, 32 to 63, ...) at most 8 rows name the same one
- neighbour_ids: int32 [512, 64], replicated, may hold values from 0 to 127, all different within a row
- resident_vectors: bfloat16 [128, 192, 1024], P('post', None, 'rep'), may hold values from -6 to 6
- resident_centroids: bfloat16 [128, 1024], P('post', 'rep'), may hold values from -1 to 1
- resident_lengths: int32 [128], P('post'), may hold values from 1 to 192
Outputs:
- new_postings: bfloat16 [256, 8, 96, 1024], P('post', None, None, 'rep')
- new_centroids: float32 [512, 2, 1024], P('post', None, 'rep')
- rescore: float32 [128, 192], P('post')
Inputs may be any that keep to these rules, and one draw needn't show every extreme that they name: `split_labels`: rows at or past a posting's length carry label 1; each half of a split posting holds between 48 and 96 valid rows, and some split has both halves of exactly 96 rows. `new_owners`: the two halves of a split go to different owners; the halves of the splits of one index of post give at most 8 to any one owner. `neighbour_ids`: each split names 64 different postings.
All inputs are finite; a program needn't handle non-finite values.
Results may differ from a plain program's by a relative error of at most 0.0034.
Values may be sent and summed in bfloat16 or wider, within the bound.
A program may use at most 128 MiB of HBM per device.

v0:
```python
import math

import jax
import jax.numpy as jnp
from jax import lax
from jax.sharding import PartitionSpec as P

D = 1024


far_value = 1e30


def nearest(best_dist, gathered, piece_start, row_data, row_norm, row_onehot, named_table):
    total_cents = gathered.shape[0]
    for block_start in range(0, total_cents, 512):
        block_width = min(512, total_cents - block_start)
        cent_block = gathered[block_start : block_start + block_width]
        cross = lax.dot_general(
            row_data, cent_block, (((1,), (1,)), ((), ())), preferred_element_type=jnp.float32
        )
        block_norm = jnp.einsum(
            "cd,cd->c", cent_block, cent_block, preferred_element_type=jnp.float32
        )
        distance = row_norm[:, None] - 2.0 * cross + block_norm[None, :]
        named_block = lax.dynamic_slice_in_dim(
            named_table, piece_start + block_start, block_width, 1
        )
        row_hits = jnp.dot(row_onehot, named_block, preferred_element_type=jnp.float32)
        distance = jnp.where(row_hits > 0.5, distance, far_value)
        best_dist = jnp.minimum(best_dist, jnp.min(distance, axis=1))
    return best_dist


def body(
    split_vectors,
    split_labels,
    split_lengths,
    new_owners,
    neighbour_ids,
    resident_vectors,
    resident_centroids,
    resident_lengths,
):
    n_post = lax.axis_size("post")
    s_local, length, dim_share = split_vectors.shape
    half_rows = length // 2
    hslot = max(2, 4 * s_local // n_post)
    row_ids = jnp.arange(length)
    is_valid = row_ids[None, :] < split_lengths[:, None]
    in_half = is_valid[:, None, :] & (split_labels[:, None, :] == jnp.arange(2)[None, :, None])
    member_int = in_half.astype(jnp.int32)
    half_rank = jnp.cumsum(member_int, axis=2) - member_int
    placement = in_half[:, :, None, :] & (
        half_rank[:, :, None, :] == jnp.arange(half_rows)[None, None, :, None]
    )
    packed = jnp.einsum(
        "shkr,srd->shkd",
        placement.astype(jnp.bfloat16),
        split_vectors,
        preferred_element_type=jnp.float32,
    ).astype(jnp.bfloat16)
    half_sums = jnp.einsum(
        "shr,srd->shd",
        in_half.astype(jnp.bfloat16),
        split_vectors,
        preferred_element_type=jnp.float32,
    )
    counts = jnp.sum(member_int, axis=2).astype(jnp.float32)
    new_centroids = half_sums / counts[:, :, None]
    owner_flat = new_owners.reshape(-1)
    half_order = jnp.arange(2 * s_local)
    same_owner = (owner_flat[:, None] == owner_flat[None, :]) & (
        half_order[None, :] < half_order[:, None]
    )
    slot_within = jnp.sum(same_owner.astype(jnp.int32), axis=1)
    target_slot = owner_flat * hslot + slot_within
    route_table = (jnp.arange(n_post * hslot)[:, None] == target_slot[None, :]).astype(jnp.bfloat16)
    outgoing = jnp.dot(
        route_table,
        packed.reshape(2 * s_local, half_rows * dim_share),
        preferred_element_type=jnp.float32,
    )
    outgoing = outgoing.astype(jnp.bfloat16).reshape(n_post, hslot, half_rows, dim_share)
    new_postings = lax.all_to_all(outgoing, "post", split_axis=0, concat_axis=0, tiled=True)
    res_local = resident_vectors.shape[0]
    own_diff = (
        resident_vectors.astype(jnp.float32) - resident_centroids.astype(jnp.float32)[:, None, :]
    )
    own_dist = lax.psum(jnp.sum(own_diff * own_diff, axis=2), "rep").reshape(-1)
    post_index = lax.axis_index("post")
    my_postings = post_index * res_local + jnp.arange(res_local)
    hits = jnp.any(neighbour_ids[:, :, None] == my_postings[None, None, :], axis=1)
    named_table = jnp.repeat(hits, 2, axis=0).T.astype(jnp.bfloat16)
    flat_rows = resident_vectors.reshape(res_local * length, dim_share)
    row_data = lax.all_gather(flat_rows, "rep", axis=1, tiled=True)
    row_posting = jnp.arange(res_local * length) // length
    row_norm = jnp.einsum("rd,rd->r", row_data, row_data, preferred_element_type=jnp.float32)
    row_onehot = (row_posting[:, None] == jnp.arange(res_local)[None, :]).astype(jnp.bfloat16)
    centroid_b = new_centroids.astype(jnp.bfloat16).reshape(2 * s_local, dim_share)
    all_shares = lax.all_gather(centroid_b, "post", axis=0, tiled=True)
    all_cents = lax.all_gather(all_shares, "rep", axis=1, tiled=True)
    best_dist = nearest(own_dist, all_cents, 0, row_data, row_norm, row_onehot, named_table)
    scores = (best_dist - row_norm) / math.sqrt(D)
    scores = scores.reshape(res_local, length)
    rescore = jnp.where(row_ids[None, :] < resident_lengths[:, None], scores, 0.0)
    return (new_postings, new_centroids, rescore)


def solution(mesh):
    return jax.shard_map(
        body,
        mesh=mesh,
        in_specs=(
            P("post", None, "rep"),
            P("post", None),
            P("post"),
            P("post", None),
            P(),
            P("post", None, "rep"),
            P("post", "rep"),
            P("post"),
        ),
        out_specs=(P("post", None, None, "rep"), P("post", None, "rep"), P("post", None)),
        check_vma=False,
    )
```

profile of v0, /device:TPU:15, one launch (start us, length us, event | category | flops | bytes accessed | tf_op | source)
XLA Modules:
  0.0 338.0 jit_solution(12658548075410980999)
XLA Ops:
  7.2 0.7 iota_compare_fusion.7
  7.9 0.9 convert_reduce_fusion
  8.9 1.2 reduce-window.6
  10.0 0.1 slice.20
  10.1 0.1 copy.40
  10.3 0.1 copy_bitcast_fusion
  10.4 0.1 copy.43
  10.5 4.6 %fusion.5 = bf16[32,2,96,512]{3,2,1,0:T(8,128)(2,1)S(1)} fusion(bf16[32,192,512]{2,1,0:T(8,128)(2,1)} %param.8, s32[32,2,192]{2,1,0:T(2,128)S(1)} %copy.43, pred[32,2,192]{2,1,0:T(4,128)(4,1)S(1)} %copy.38), kind=kOutput, calls=%fused_computation.7 | convolution fusion | flops 1213464576 | bytes 12644352 | tf_op jit(solution)/shard_map/shkr,srd->shkd/dot_general | solution.py:57
  15.0 0.0 copy-start.6
  15.0 6.6 %copy.63 = bf16[8,8,96,512]{3,1,2,0:T(8,128)(2,1)} copy(bf16[8,8,96,512]{3,2,1,0:T(8,128)(2,1)S(1)} %bitcast.41) | data formatting | bytes 12582912
  21.6 0.0 copy-done.6
  21.6 0.1 copy.37
  21.7 0.1 reshape.99
  21.8 0.2 convert_reduce_fusion.1
  22.0 6.4 %convolution_convert_fusion = bf16[128,49152]{1,0:T(8,128)(2,1)S(1)} fusion(bf16[64,49152]{1,0:T(8,128)(2,1)} %bitcast.42, s32[64]{0:T(128)S(1)} %multiply_add_fusion), kind=kOutput, calls=%fused_computation | convolution fusion | flops 811606016 | bytes 18874624 | tf_op jit(solution)/shard_map/dot_general | solution.py:79
  28.4 7.2 %copy.44 = bf16[16,8,96,512]{3,2,1,0:T(8,128)(2,1)} copy(bf16[16,8,96,512]{3,1,2,0:T(8,128)(2,1)S(1)} %bitcast.40) | data formatting | bytes 25165824 | tf_op jit(solution)/shard_map/reshape | solution.py:84
  35.7 6.6 %all-to-all-start = ((bf16[16,8,96,512]{3,2,1,0:T(8,128)(2,1)}), bf16[16,8,96,512]{3,2,1,0:T(8,128)(2,1)}, u32[]{:S(2)}, u32[]{:S(2)}) async-start(bf16[16,8,96,512]{3,2,1,0:T(8,128)(2,1)} %copy.44), calls=%async_computation | async-start | bytes 25165824 | tf_op jit(solution)/shard_map/all_to_all | solution.py:85
  42.2 0.0 all-gather.6.cloned.1.call-start
  42.3 0.1 copy.46
  42.4 4.4 %fusion.41 = (bf16[32,2,512]{2,1,0:T(2,128)(2,1)S(1)}, f32[32,2,512]{2,1,0:T(2,128)}) fusion(f32[32,2]{1,0:T(8,128)S(1)} %copy.46, bf16[32,192,512]{2,1,0:T(8,128)(2,1)} %param.8, pred[32,2,192]{2,0,1:T(32,128)(4,1)S(1)} %get-tuple-element.6), kind=kOutput, calls=%fused_computation.65 | convolution fusion | flops 12648448 | bytes 6500608 | tf_op jit(solution)/shard_map/shr,srd->shd/dot_general | solution.py:63
  46.8 0.6 reshape.107
  47.4 0.0 all-gather.6.cloned.1.call-update
  47.4 0.0 all-gather.4.cloned.1.call-start
  47.5 0.7 all-gather.4.cloned.1.call-update
  48.2 0.0 all-gather.8.cloned.1.call-start
  48.2 162.0 %all-gather.6.cloned.1.call-done = bf16[1024,512]{1,0:T(8,128)(2,1)} async-done(((bf16[64,512]{1,0:T(8,128)(2,1)}), bf16[1024,512]{1,0:T(8,128)(2,1)}) %all-gather.6.cloned.1.call-update) | async-done | bytes 1048592 | tf_op jit(solution)/shard_map/all_gather | solution.py:101
  210.2 0.0 all-gather.8.cloned.1.call-update
  210.3 0.2 compare_reduce_fusion
  210.5 0.2 copy.47
  210.7 0.2 broadcast_in_dim.9
  210.9 0.3 reshape.105
  211.2 0.0 copy-done.5
  211.3 0.5 multiply_reduce_fusion
  211.8 0.1 reshape.104
  211.8 4.2 %psum.7 = f32[1536]{0:T(1024)S(1)} all-reduce(f32[1536]{0:T(1024)S(1)} %reshape.104), channel_id=1, replica_groups=mesh['post'=16,'rep'=2] {'rep'}, use_global_device_ids=true, to_apply=%region_5.6 | all-reduce | flops 1536 | bytes 12288 | tf_op jit(solution)/shard_map/psum | solution.py:90
  216.1 2.4 fusion.26
  218.4 2.4 fusion.27
  220.8 45.5 %all-gather.4.cloned.1.call-done = bf16[1536,1024]{1,0:T(8,128)(2,1)} async-done(((bf16[1536,512]{1,0:T(8,128)(2,1)}), bf16[1536,1024]{1,0:T(8,128)(2,1)}) %all-gather.4.cloned.1.call-update) | async-done | bytes 3145744 | tf_op jit(solution)/shard_map/all_gather | solution.py:96
  266.4 2.7 fusion.2
  269.1 32.0 %all-gather.8.cloned.1.call-done = bf16[1024,1024]{1,0:T(8,128)(2,1)} async-done(((bf16[1024,512]{1,0:T(8,128)(2,1)}), bf16[1024,1024]{1,0:T(8,128)(2,1)}) %all-gather.8.cloned.1.call-update) | async-done | bytes 2097168 | tf_op jit(solution)/shard_map/all_gather | solution.py:102
  301.1 2.0 fusion.21
  303.1 4.4 %fusion.23 = f32[1536]{0:T(1024)S(1)} fusion(f32[512]{0:T(512)S(1)} %get-tuple-element.4, bf16[1536,1024]{1,0:T(8,128)(2,1)S(1)} %copy-done.1, f32[1536]{0:T(1024)S(1)} %fusion.2, f32[1536,512]{0,1:T(8,128)} %fusion.26, bf16[1024,1024]{1,0:T(8,128)(2,1)} %all-gather.8.cloned.1.call-done), kind=kOutput, calls=%fused_computation.26 | convolution fusion | flops 1615329792 | bytes 7354368 | tf_op jit(solution)/shard_map/dot_general | solution.py:19
  307.6 0.0 copy-start.7
  307.6 2.1 fusion.22
  309.7 0.1 reshape.108
  309.8 0.7 fusion.37
  310.4 10.3 %all-to-all-done = bf16[16,8,96,512]{3,2,1,0:T(8,128)(2,1)} async-done(((bf16[16,8,96,512]{3,2,1,0:T(8,128)(2,1)}), bf16[16,8,96,512]{3,2,1,0:T(8,128)(2,1)}, u32[]{:S(2)}, u32[]{:S(2)}) %all-to-all-start) | async-done | bytes 12582944 | tf_op jit(solution)/shard_map/all_to_all | solution.py:85
  320.8 10.8 %copy.72 = bf16[16,8,96,512]{3,2,1,0:T(8,128)(2,1)} copy(bf16[16,8,96,512]{3,2,1,0:T(8,128)(2,1)} %all-to-all-done) | data formatting | bytes 25165824
  (25 shorter events, 0.2 us)
Async XLA Ops:
  15.0 6.6 %copy-start.6 = (s32[32,2]{0,1:T(2,128)S(1)}, s32[32,2]{0,1:T(2,128)}, u32[]{:S(2)}) copy-start(s32[32,2]{0,1:T(2,128)} %param.11) | copy-start | bytes 772
  35.7 285.1 %all-to-all-start = ((bf16[16,8,96,512]{3,2,1,0:T(8,128)(2,1)}), bf16[16,8,96,512]{3,2,1,0:T(8,128)(2,1)}, u32[]{:S(2)}, u32[]{:S(2)}) async-start(bf16[16,8,96,512]{3,2,1,0:T(8,128)(2,1)} %copy.44), calls=%async_computation | async-start | bytes 25165824 | tf_op jit(solution)/shard_map/all_to_all | solution.py:85
  42.2 168.0 %all-gather.6.cloned.1.call-start = ((), (), s32[]{:S(2)}) async-start(), calls=%async_computation.2 | async-start | bytes 1114112 | tf_op jit(solution)/shard_map/all_gather | solution.py:101
  42.4 167.9 %copy-start.4 = (s32[512,64]{0,1:T(8,128)S(1)}, s32[512,64]{0,1:T(8,128)}, u32[]{:S(2)}) copy-start(s32[512,64]{0,1:T(8,128)} %param.12) | copy-start | bytes 393220
  46.8 164.5 %copy-start.5 = (bf16[8,512]{1,0:T(8,128)(2,1)S(1)}, bf16[8,512]{1,0:T(8,128)(2,1)}, u32[]{:S(2)}) copy-start(bf16[8,512]{1,0:T(8,128)(2,1)} %param.14) | copy-start | bytes 24580
  46.8 164.5 %copy-start = (bf16[8,192,512]{2,1,0:T(8,128)(2,1)S(1)}, bf16[8,192,512]{2,1,0:T(8,128)(2,1)}, u32[]{:S(2)}) copy-start(bf16[8,192,512]{2,1,0:T(8,128)(2,1)} %param.13) | copy-start | bytes 4718596
  47.4 218.9 %all-gather.4.cloned.1.call-start = ((), (), s32[]{:S(2)}) async-start(), calls=%async_computation.1 | async-start | bytes 4718592 | tf_op jit(solution)/shard_map/all_gather | solution.py:96
  48.2 252.9 %all-gather.8.cloned.1.call-start = ((), (), s32[]{:S(2)}) async-start(), calls=%async_computation.3 | async-start | bytes 3145728 | tf_op jit(solution)/shard_map/all_gather | solution.py:102
  266.4 36.7 %copy-start.1 = (bf16[1536,1024]{1,0:T(8,128)(2,1)S(1)}, bf16[1536,1024]{1,0:T(8,128)(2,1)}, u32[]{:S(2)}) copy-start(bf16[1536,1024]{1,0:T(8,128)(2,1)} %all-gather.4.cloned.1.call-done) | copy-start | bytes 9437188
  303.1 4.5 %copy-start.2 = (f32[1536,512]{0,1:T(8,128)S(1)}, f32[1536,512]{0,1:T(8,128)}, u32[]{:S(2)}) copy-start(f32[1536,512]{0,1:T(8,128)} %fusion.27) | copy-start | bytes 9437188
  303.1 4.5 %copy-start.3 = (bf16[1024,1024]{1,0:T(8,128)(2,1)S(1)}, bf16[1024,1024]{1,0:T(8,128)(2,1)}, u32[]{:S(2)}) copy-start(bf16[1024,1024]{1,0:T(8,128)(2,1)} %all-gather.8.cloned.1.call-done) | copy-start | bytes 6291460
  307.6 2.2 copy-start.7
Sparse Core Ops, SparseCore 0:
  47.6 162.6 all-gather.5
  211.8 54.5 all-gather.3
  267.9 33.1 all-gather.7
where the time goes:
time: 339 us; the launch traced here: 338 us
  waiting for transfers between devices  251 us (74%)
  local copies, waits for them, and re-layouts  26.7 us (8%)
  matrix products  26.6 us (8%)
  between operations  14 us (4%)
  other arithmetic  9.28 us (3%)
  starting transfers between devices  6.67 us (2%)
  blocking collectives  4.23 us (1%)
    all_gather x1, waiting for transfers between devices, body(): all_shares = lax.all_gather(centroid_b, 'post', axis=0, tiled=True)  162 us
    all_gather x1, waiting for transfers between devices, body(): row_data = lax.all_gather(flat_rows, 'rep', axis=1, tiled=True)  45.5 us
    all_gather x1, waiting for transfers between devices, body(): all_cents = lax.all_gather(all_shares, 'rep', axis=1, tiled=True)  32 us
    unnamed x19, local copies, waits for them, and re-layouts  17.5 us
    all_to_all x1, waiting for transfers between devices, body(): lax.all_to_all(outgoing, 'post', split_axis=0, concat_axis=0, tiled=True)  10.3 us
    reshape x1, local copies, waits for them, and re-layouts, body(): outgoing.astype(jnp.bfloat16).reshape(n_post, hslot, half_rows, dim_share)  7.23 us
  transfers between devices with their start and end apart: 4, of which 4 were waited for; matrix products, arithmetic and copies ran while one was open for 7% of the time, Pallas kernels for 0%

commit v1 on v0

v1 whole, which is shorter than its diff:
```python
import functools
import math

import jax
import jax.numpy as jnp
from jax import lax
from jax.experimental import pallas as pl
from jax.experimental.pallas import tpu as pltpu
from jax.sharding import PartitionSpec as P

far_value = 1e30
STEP = 8


def pack_kernel(
    n_halves, n_slots, target_ref, empty_ref, vec_ref, label_ref, length_ref, out_ref, cent_ref, packed, blank, sem
):
    step = pl.program_id(0)
    length = vec_ref.shape[1]
    half_rows = length // 2

    @pl.when(step == 0)
    def _():
        blank[...] = jnp.zeros_like(blank)

        def clear(i, carry):
            pltpu.make_async_copy(blank, out_ref.at[empty_ref[i]], sem).start()
            return carry

        lax.fori_loop(0, n_slots - n_halves, clear, 0)

    labels = label_ref[...]
    valid = lax.broadcasted_iota(jnp.int32, labels.shape, 1) < length_ref[...]
    first = jnp.where(valid & (labels == 0), 1.0, 0.0)
    second = jnp.where(valid & (labels == 1), 1.0, 0.0)
    earlier = lax.broadcasted_iota(jnp.int32, (length, length), 0) < lax.broadcasted_iota(
        jnp.int32, (length, length), 1
    )
    earlier = jnp.where(earlier, 1.0, 0.0).astype(jnp.bfloat16)
    rank_first = jnp.dot(first.astype(jnp.bfloat16), earlier, preferred_element_type=jnp.float32)
    rank_second = jnp.dot(second.astype(jnp.bfloat16), earlier, preferred_element_type=jnp.float32)
    place = jnp.where(first > 0, rank_first, jnp.where(second > 0, half_rows + rank_second, -1.0))
    place = place.astype(jnp.int32)
    count_first = jnp.sum(first, axis=1, keepdims=True)
    count_second = jnp.sum(second, axis=1, keepdims=True)
    row = lax.broadcasted_iota(jnp.int32, (length + 16, length), 0)
    for s in range(STEP):
        chosen = jnp.where(row == place[s : s + 1], 1.0, 0.0)
        chosen = jnp.where(row == length, first[s : s + 1], chosen)
        chosen = jnp.where(row == length + 1, second[s : s + 1], chosen)
        rows = jnp.dot(chosen.astype(jnp.bfloat16), vec_ref[s], preferred_element_type=jnp.float32)
        cent_ref[2 * s : 2 * s + 1] = rows[length : length + 1] / count_first[s : s + 1]
        cent_ref[2 * s + 1 : 2 * s + 2] = rows[length + 1 : length + 2] / count_second[s : s + 1]
        half = (step * STEP + s) * 2
        for h in range(2):
            packed[half + h] = rows[h * half_rows : (h + 1) * half_rows].astype(jnp.bfloat16)
            pltpu.make_async_copy(packed.at[half + h], out_ref.at[target_ref[half + h]], sem).start()

    @pl.when(step == pl.num_programs(0) - 1)
    def _():
        pltpu.make_async_copy(out_ref, out_ref, sem).wait()


def pack(vectors, labels, lengths, target, empty, n_slots):
    s_local, length, dim_share = vectors.shape
    half_rows = length // 2
    return pl.pallas_call(
        functools.partial(pack_kernel, 2 * s_local, n_slots),
        grid_spec=pltpu.PrefetchScalarGridSpec(
            num_scalar_prefetch=2,
            grid=(s_local // STEP,),
            in_specs=[
                pl.BlockSpec((STEP, length, dim_share), lambda i, *_: (i, 0, 0)),
                pl.BlockSpec((STEP, length), lambda i, *_: (i, 0)),
                pl.BlockSpec((STEP, 1), lambda i, *_: (i, 0)),
            ],
            out_specs=[
                pl.BlockSpec(memory_space=pl.ANY),
                pl.BlockSpec((2 * STEP, dim_share), lambda i, *_: (i, 0)),
            ],
            scratch_shapes=[
                pltpu.VMEM((2 * s_local, half_rows, dim_share), jnp.bfloat16),
                pltpu.VMEM((half_rows, dim_share), jnp.bfloat16),
                pltpu.SemaphoreType.DMA,
            ],
        ),
        out_shape=[
            jax.ShapeDtypeStruct((n_slots, half_rows, dim_share), jnp.bfloat16),
            jax.ShapeDtypeStruct((2 * s_local, dim_share), jnp.float32),
        ],
        compiler_params=pltpu.CompilerParams(vmem_limit_bytes=32 * 2**20),
        cost_estimate=pl.CostEstimate(
            flops=2 * s_local * (length + 16) * length * dim_share,
            bytes_accessed=2 * vectors.size + 2 * n_slots * half_rows * dim_share,
            transcendentals=0,
        ),
    )(target, empty, vectors, labels, lengths[:, None])


def routes(new_owners, n_post, hslot):
    owner_flat = new_owners.reshape(-1)
    n_halves = owner_flat.shape[0]
    n_slots = n_post * hslot
    half_order = jnp.arange(n_halves)
    same_owner = (owner_flat[:, None] == owner_flat[None, :]) & (
        half_order[None, :] < half_order[:, None]
    )
    slot_within = jnp.sum(same_owner.astype(jnp.int32), axis=1)
    target = owner_flat * hslot + slot_within
    slot_ids = jnp.arange(n_slots)
    is_empty = ~jnp.any(slot_ids[:, None] == target[None, :], axis=1)
    before = jnp.sum((is_empty[None, :] & (slot_ids[None, :] < slot_ids[:, None])).astype(jnp.int32), axis=1)
    chosen = is_empty[None, :] & (before[None, :] == jnp.arange(n_slots - n_halves)[:, None])
    empty = jnp.sum(jnp.where(chosen, slot_ids[None, :], 0), axis=1)
    return target.astype(jnp.int32), empty.astype(jnp.int32)


def body(
    split_vectors,
    split_labels,
    split_lengths,
    new_owners,
    neighbour_ids,
    resident_vectors,
    resident_centroids,
    resident_lengths,
):
    n_post = lax.axis_size("post")
    s_local, length, dim_share = split_vectors.shape
    half_rows = length // 2
    hslot = max(2, 4 * s_local // n_post)
    res_local = resident_vectors.shape[0]
    n_rep = lax.axis_size("rep")
    res_part = res_local // n_rep
    post_index = lax.axis_index("post")
    rep_index = lax.axis_index("rep")
    mine_at = rep_index * res_part

    def shifted(array, offset):
        if offset == 0:
            return array
        return lax.ppermute(array, "rep", [(i, (i + offset) % n_rep) for i in range(n_rep)])

    def part_of(array, offset):
        at = lax.rem(rep_index + offset, n_rep) * res_part
        return lax.dynamic_slice_in_dim(array, at, res_part, 0)

    rows_shares = [shifted(part_of(resident_vectors, k), k) for k in range(n_rep)]
    current_shares = [shifted(part_of(resident_centroids, k), k) for k in range(n_rep)]

    target, empty = routes(new_owners, n_post, hslot)
    outgoing, centroids = pack(split_vectors, split_labels, split_lengths, target, empty, n_post * hslot)
    new_centroids = centroids.reshape(s_local, 2, dim_share)
    cent_mine = lax.all_gather(centroids.astype(jnp.bfloat16), "post", axis=0, tiled=True)
    outgoing, cent_mine = lax.optimization_barrier((outgoing, cent_mine))
    outgoing = outgoing.reshape(n_post, hslot, half_rows, dim_share)
    new_postings = lax.all_to_all(outgoing, "post", split_axis=0, concat_axis=0, tiled=True)

    cent_shares = [shifted(cent_mine, k) for k in range(n_rep)]
    n_cents = cent_mine.shape[0]
    my_postings = post_index * res_local + mine_at + jnp.arange(res_part)
    hits = jnp.any(neighbour_ids[:, :, None] == my_postings[None, None, :], axis=1)
    hits = jnp.repeat(hits, 2, axis=0).T

    own = 0.0
    row_norm = 0.0
    cent_norm = 0.0
    cross = 0.0
    for rows, current, cents in zip(rows_shares, current_shares, cent_shares):
        wide = rows.astype(jnp.float32)
        gap = wide - current.astype(jnp.float32)[:, None, :]
        own += jnp.sum(gap * gap, axis=2)
        row_norm += jnp.sum(wide * wide, axis=2)
        cents_wide = cents.astype(jnp.float32)
        cent_norm += jnp.sum(cents_wide * cents_wide, axis=1)
        cross += lax.dot_general(
            rows.reshape(res_part * length, dim_share),
            cents,
            (((1,), (1,)), ((), ())),
            preferred_element_type=jnp.float32,
        )
    distance = row_norm[:, :, None] - 2.0 * cross.reshape(res_part, length, n_cents) + cent_norm
    distance = jnp.where(hits[:, None, :], distance, far_value)
    best_dist = jnp.minimum(own, jnp.min(distance, axis=2))
    scores = (best_dist - row_norm) / math.sqrt(n_rep * dim_share)
    lengths_mine = part_of(resident_lengths, 0)
    scores = jnp.where(jnp.arange(length)[None, :] < lengths_mine[:, None], scores, 0.0)
    rescore = lax.all_gather(scores, "rep", axis=0, tiled=True)
    return (new_postings, new_centroids, rescore)


def solution(mesh):
    return jax.shard_map(
        body,
        mesh=mesh,
        in_specs=(
            P("post", None, "rep"),
            P("post", None),
            P("post"),
            P("post", None),
            P(),
            P("post", None, "rep"),
            P("post", "rep"),
            P("post"),
        ),
        out_specs=(P("post", None, None, "rep"), P("post", None, "rep"), P("post", None)),
        check_vma=False,
    )
```

time: 339 us -> 379 us (1.12)
  waiting for transfers between devices: 251 us -> 295 us
  Pallas kernels: 0 us -> 24.8 us
  matrix products: 26.6 us -> 3.45 us
  other arithmetic: 9.28 us -> 4.77 us
    all_to_all x1, waiting for transfers between devices: 10.3 us -> 224 us  [body(): lax.all_to_all(outgoing, 'post', split_axis=0, concat_axis=0, tiled=True)]
    all_gather x3 -> x1, waiting for transfers between devices: 240 us -> 38.4 us  [body(): lax.all_gather(centroids.astype(jnp.bfloat16), 'post', axis=0, tiled=True)]
    ppermute x0 -> x3, waiting for transfers between devices: none -> 32.5 us  [shifted(): lax.ppermute(array, 'rep', [(i, (i + offset) % n_rep) for i in range(n_re...]
    pallas_call x0 -> x1, Pallas kernels: none -> 24.8 us  [pack(): pl.pallas_call(functools.partial(pack_kernel, 2 * s_local, n_slots), grid...]
    dot_general x7 -> x2, matrix products: 26.6 us -> 3.45 us  [body(): lax.dot_general(rows.reshape(res_part * length, dim_share), cents, (((1,)...]
    reshape x7 -> x3, local copies, waits for them, and re-layouts: 8.44 us -> 1.51 us  [the longest x1 0.73 us: body(): new_centroids = centroids.reshape(s_local, 2, dim_share)]
    dot_general x2 -> x0, other arithmetic: 4.74 us -> none  [the longest x1 2.72 us: body(): jnp.einsum('rd,rd->r', row_data, row_data, preferred_element_type=jnp.flo...]
    psum x1 -> x0, blocking collectives: 4.23 us -> none  [body(): own_dist = lax.psum(jnp.sum(own_diff * own_diff, axis=2), 'rep').reshape(-1)]
  transfers between devices with their start and end apart: 4 -> 5, of which waited for: 4 -> 4; matrix products, arithmetic and copies ran while one was open for 7% -> 3% of each run, Pallas kernels for 0% -> 0%
where the time goes in v1:
time: 379 us; the launch traced here: 378 us
  waiting for transfers between devices  295 us (78%)
  Pallas kernels  24.8 us (7%)
  local copies, waits for them, and re-layouts  24.2 us (6%)
  between operations  14.2 us (4%)
  starting transfers between devices  8.46 us (2%)
  other arithmetic  4.77 us (1%)
    all_to_all x1, waiting for transfers between devices, body(): lax.all_to_all(outgoing, 'post', split_axis=0, concat_axis=0, tiled=True)  224 us
    all_gather x1, waiting for transfers between devices, body(): lax.all_gather(centroids.astype(jnp.bfloat16), 'post', axis=0, tiled=True)  38.4 us
    ppermute x3, waiting for transfers between devices, shifted(): lax.ppermute(array, 'rep', [(i, (i + offset) % n_rep) for i in range(n_re...  32.5 us
    pallas_call x1, Pallas kernels, pack(): pl.pallas_call(functools.partial(pack_kernel, 2 * s_local, n_slots), grid...  24.8 us
    unnamed x19, local copies, waits for them, and re-layouts  20.5 us
  transfers between devices with their start and end apart: 5, of which 4 were waited for; matrix products, arithmetic and copies ran while one was open for 3% of the time, Pallas kernels for 0%

profile of v1, /device:TPU:15, one launch (start us, length us, event | category | flops | bytes accessed | tf_op | source)
XLA Modules:
  0.0 378.0 jit_solution(6269718581086432147)
XLA Ops:
  7.2 0.0 all-gather.3.cloned.1.call-start
  7.2 0.8 copy.20
  8.0 0.1 reshape.65
  8.1 0.2 convert_reduce_fusion.1
  8.3 0.1 fusion.8
  8.4 0.1 convert_reduce_fusion
  8.5 0.1 select_reduce_fusion.1.empty_ref
  8.6 0.7 copy.21.length_ref
  9.4 2.8 copy-done.1
  12.1 0.8 copy-done.2
  12.9 24.8 %shard_map.103 = (bf16[128,96,512]{2,1,0:T(8,128)(2,1)S(1)}, f32[64,512]{1,0:T(8,128)S(1)}) custom-call(s32[64]{0:T(128)S(1)} %multiply_add_fusion.target_ref, s32[64]{0:T(128)S(1)} %select_reduce_fusion.1.empty_ref, bf16[32,192,512]{2,1,0:T(8,128)(2,1)S(1)} %copy-done.1, s32[32,192]{1,0:T(8,128)S(1)} %copy-done.2, s32[32,1]{1,0:T(8,128)S(1)} %copy.21.length_ref), custom_call_target="tpu_custom_call" | custom-call | flops 1308622848 | bytes 18874368 | tf_op jit(solution)/shard_map/pallas_call | solution.py:67
  37.7 0.0 copy-start
  37.7 4.8 %copy-done = bf16[128,96,512]{2,1,0:T(8,128)(2,1)} copy-done((bf16[128,96,512]{2,1,0:T(8,128)(2,1)}, bf16[128,96,512]{2,1,0:T(8,128)(2,1)S(1)}, u32[]{:S(2)}) %copy-start) | copy-done | bytes 12582936
  42.5 0.6 convert_element_type.29
  43.1 0.0 all-gather.3.cloned.1.call-update
  43.1 38.4 %all-gather.3.cloned.1.call-done = bf16[1024,512]{1,0:T(8,128)(2,1)} async-done(((bf16[64,512]{1,0:T(8,128)(2,1)}), bf16[1024,512]{1,0:T(8,128)(2,1)}) %all-gather.3.cloned.1.call-update) | async-done | bytes 1048592 | tf_op jit(solution)/shard_map/all_gather | solution.py:154
  81.5 6.6 %all-to-all-start = ((bf16[16,8,96,512]{3,2,1,0:T(8,128)(2,1)}), bf16[16,8,96,512]{3,2,1,0:T(8,128)(2,1)}, u32[]{:S(2)}, u32[]{:S(2)}) async-start(bf16[16,8,96,512]{3,2,1,0:T(8,128)(2,1)} %bitcast.15), calls=%async_computation | async-start | bytes 25165824 | tf_op jit(solution)/shard_map/all_to_all | solution.py:157
  88.1 0.0 copy-start.7
  88.2 0.0 copy-done.4
  88.2 0.9 constant_dynamic-slice_fusion
  89.1 0.3 collective-permute-start
  89.4 0.0 copy-done.6
  89.4 1.3 collective-permute-start.1
  90.7 0.0 copy-done.3
  90.7 0.3 collective-permute-start.2
  91.0 2.4 fusion.1
  93.3 0.0 copy-done.5
  93.3 0.1 compare_reduce_fusion
  93.5 0.7 reshape.67
  94.2 0.3 broadcast_in_dim.36
  94.6 0.7 reshape.68
  95.3 0.0 copy-done.7
  95.3 0.1 dynamic_slice.15
  95.3 13.0 %collective-permute-done.1 = bf16[4,512]{1,0:T(4,128)(2,1)S(1)} collective-permute-done((bf16[4,512]{1,0:T(4,128)(2,1)S(1)}, bf16[4,512]{1,0:T(4,128)(2,1)S(1)}, u32[]{:S(2)}, u32[]{:S(2)}) %collective-permute-start.1) | collective-permute-done | bytes 4128 | tf_op jit(solution)/shard_map/ppermute | solution.py:142
  108.3 0.0 collective-permute-done
  108.3 0.4 fusion.4
  108.7 0.1 add.70
  108.8 0.3 multiply_reduce_fusion.1
  109.1 2.1 fusion.10
  111.3 19.5 %collective-permute-done.2 = bf16[1024,512]{1,0:T(8,128)(2,1)S(1)} collective-permute-done((bf16[1024,512]{1,0:T(8,128)(2,1)S(1)}, bf16[1024,512]{1,0:T(8,128)(2,1)S(1)}, u32[]{:S(2)}, u32[]{:S(2)}) %collective-permute-start.2) | collective-permute-done | bytes 1048608 | tf_op jit(solution)/shard_map/ppermute | solution.py:142
  130.8 0.3 multiply_reduce_fusion
  131.1 1.3 select_reduce_fusion
  132.4 0.1 reduce_min.12
  132.4 0.1 select_bitcast_fusion
  132.5 3.5 all-gather
  136.0 0.6 reshape.72
  136.6 223.8 %all-to-all-done = bf16[16,8,96,512]{3,2,1,0:T(8,128)(2,1)} async-done(((bf16[16,8,96,512]{3,2,1,0:T(8,128)(2,1)}), bf16[16,8,96,512]{3,2,1,0:T(8,128)(2,1)}, u32[]{:S(2)}, u32[]{:S(2)}) %all-to-all-start) | async-done | bytes 12582944 | tf_op jit(solution)/shard_map/all_to_all | solution.py:157
  360.4 10.8 %copy.23 = bf16[16,8,96,512]{3,2,1,0:T(8,128)(2,1)} copy(bf16[16,8,96,512]{3,2,1,0:T(8,128)(2,1)} %all-to-all-done) | data formatting | bytes 25165824
  (13 shorter events, 0.0 us)
Async XLA Ops:
  7.2 74.3 %all-gather.3.cloned.1.call-start = ((), (), s32[]{:S(2)}) async-start(), calls=%async_computation.1 | async-start | bytes 1114112 | tf_op jit(solution)/shard_map/all_gather | solution.py:154
  9.4 2.8 copy-start.1
  12.1 0.8 copy-start.2
  37.7 4.8 %copy-start = (bf16[128,96,512]{2,1,0:T(8,128)(2,1)}, bf16[128,96,512]{2,1,0:T(8,128)(2,1)S(1)}, u32[]{:S(2)}) copy-start(bf16[128,96,512]{2,1,0:T(8,128)(2,1)S(1)} %get-tuple-element.9) | copy-start | bytes 37748740
  81.5 6.7 %copy-start.4 = (bf16[8,192,512]{2,1,0:T(8,128)(2,1)S(1)}, bf16[8,192,512]{2,1,0:T(8,128)(2,1)}, u32[]{:S(2)}) copy-start(bf16[8,192,512]{2,1,0:T(8,128)(2,1)} %param.13) | copy-start | bytes 4718596
  81.5 7.9 %copy-start.6 = (bf16[8,512]{1,0:T(8,128)(2,1)S(1)}, bf16[8,512]{1,0:T(8,128)(2,1)}, u32[]{:S(2)}) copy-start(bf16[8,512]{1,0:T(8,128)(2,1)} %param.14) | copy-start | bytes 24580
  81.5 9.2 %copy-start.3 = (bf16[1024,512]{1,0:T(8,128)(2,1)S(1)}, bf16[1024,512]{1,0:T(8,128)(2,1)}, u32[]{:S(2)}) copy-start(bf16[1024,512]{1,0:T(8,128)(2,1)} %all-gather.3.cloned.1.call-done) | copy-start | bytes 3145732
  81.5 278.9 %all-to-all-start = ((bf16[16,8,96,512]{3,2,1,0:T(8,128)(2,1)}), bf16[16,8,96,512]{3,2,1,0:T(8,128)(2,1)}, u32[]{:S(2)}, u32[]{:S(2)}) async-start(bf16[16,8,96,512]{3,2,1,0:T(8,128)(2,1)} %bitcast.15), calls=%async_computation | async-start | bytes 25165824 | tf_op jit(solution)/shard_map/all_to_all | solution.py:157
  88.1 5.2 %copy-start.5 = (s32[512,64]{0,1:T(8,128)S(1)}, s32[512,64]{0,1:T(8,128)}, u32[]{:S(2)}) copy-start(s32[512,64]{0,1:T(8,128)} %param.12) | copy-start | bytes 393220
  88.1 7.1 %copy-start.7 = (s32[8]{0:T(128)S(1)}, s32[8]{0:T(128)}, u32[]{:S(2)}) copy-start(s32[8]{0:T(128)} %param.15) | copy-start | bytes 100
  89.1 19.2 %collective-permute-start = (bf16[4,192,512]{2,1,0:T(8,128)(2,1)}, bf16[4,192,512]{2,1,0:T(8,128)(2,1)S(1)}, u32[]{:S(2)}, u32[]{:S(2)}) collective-permute-start(bf16[4,192,512]{2,1,0:T(8,128)(2,1)} %constant_dynamic-slice_fusion), channel_id=1, source_target_pairs={{0,1},{1,0},{2,3},{3,2},{4,5},{5,4},{6,7},{7,6},{8,9},{9,8},{10,11... | collective-permute-start | bytes 2359304 | tf_op jit(solution)/shard_map/ppermute | solution.py:142
  89.4 18.9 %collective-permute-start.1 = (bf16[4,512]{1,0:T(4,128)(2,1)S(1)}, bf16[4,512]{1,0:T(4,128)(2,1)S(1)}, u32[]{:S(2)}, u32[]{:S(2)}) collective-permute-start(bf16[4,512]{1,0:T(4,128)(2,1)S(1)} %get-tuple-element.16), channel_id=1, source_target_pairs={{0,1},{1,0},{2,3},{3,2},{4,5},{5,4},{6,7},{7,6},{8,9},{9,8},{10,11... | collective-permute-start | bytes 12296 | tf_op jit(solution)/shard_map/ppermute | solution.py:142
  90.7 40.1 %collective-permute-start.2 = (bf16[1024,512]{1,0:T(8,128)(2,1)S(1)}, bf16[1024,512]{1,0:T(8,128)(2,1)S(1)}, u32[]{:S(2)}, u32[]{:S(2)}) collective-permute-start(bf16[1024,512]{1,0:T(8,128)(2,1)S(1)} %copy-done.3), channel_id=1, source_target_pairs={{0,1},{1,0},{2,3},{3,2},{4,5},{5,4},{6,7},{7,6},{8,9},{9,8},{10,11... | collective-permute-start | bytes 3145736 | tf_op jit(solution)/shard_map/ppermute | solution.py:142
Sparse Core Ops, SparseCore 0:
  43.3 38.2 all-gather.2

commit v2 on v1

v2 whole, which is shorter than its diff:
```python
import functools
import math

import jax
import jax.numpy as jnp
from jax import lax
from jax.experimental import pallas as pl
from jax.experimental.pallas import tpu as pltpu
from jax.sharding import PartitionSpec as P

far_value = 1e30
ROWS = 16
GROUP = 4
MESH = pl.DeviceIdType.MESH


def wait_bytes(ref, sem):
    pltpu.make_async_copy(ref, ref, sem).wait()


def exchange_kernel(
    cross_ref,
    near_ref,
    relay_ref,
    vec_ref,
    label_ref,
    length_ref,
    out_ref,
    cent_ref,
    cent_all,
    cent_rep,
    packed,
    place,
    members,
    cross_send,
    near_send,
    relay_send,
    cent_own,
    cent_in,
    cross_sem,
    near_sem,
    relay_sem,
    out_sem,
    cent_sem,
    cent_fwd_sem,
    cent_in_sem,
    cent_all_sem,
    rep_sem,
    rep_in_sem,
    cross_in_sem,
    *cross_in,
):
    n_post = lax.axis_size("post")
    n_rep = lax.axis_size("rep")
    me = lax.axis_index("post")
    rep = lax.axis_index("rep")
    lanes = n_post // 4
    peers = n_post // 2
    side = me // peers
    base = side * peers
    layer = me // lanes
    lane = lax.rem(me, lanes)
    turn = lax.rem(layer, 2)
    relay = (2 - side) * lanes + lane
    is_relay = (layer == 1) | (layer == 2)
    first_source = (1 - side) * peers + lane
    s_local, length, dim_share = vec_ref.shape
    half_rows = length // 2
    n_halves = 2 * s_local
    hslot = out_ref.shape[1]
    capacity = cross_send.shape[1]
    chunks = half_rows // ROWS

    def peer(k):
        return base + lax.rem(me - base + k, peers)

    def post_id(p):
        return {"post": p}

    def rep_id(k):
        return {"rep": lax.rem(rep + k, n_rep)}

    barrier = pltpu.get_barrier_semaphore()

    def greet(k, carry):
        pl.semaphore_signal(barrier, inc=1, device_id=post_id(peer(k)), device_id_type=MESH)
        return carry

    lax.fori_loop(1, peers, greet, 0)
    for k in range(1, n_rep):
        pl.semaphore_signal(barrier, inc=1, device_id=rep_id(k), device_id_type=MESH)

    @pl.when(is_relay)
    def _():
        for j in range(2):
            pl.semaphore_signal(
                barrier, inc=1, device_id=post_id(first_source + j * lanes), device_id_type=MESH
            )

    labels = label_ref[...]
    valid = lax.broadcasted_iota(jnp.int32, labels.shape, 1) < length_ref[...]
    first = jnp.where(valid & (labels == 0), 1.0, 0.0)
    second = jnp.where(valid & (labels == 1), 1.0, 0.0)
    earlier = lax.broadcasted_iota(jnp.int32, (length, length), 0) < lax.broadcasted_iota(
        jnp.int32, (length, length), 1
    )
    earlier = jnp.where(earlier, 1.0, 0.0).astype(jnp.bfloat16)
    rank_first = jnp.dot(first.astype(jnp.bfloat16), earlier, preferred_element_type=jnp.float32)
    rank_second = jnp.dot(second.astype(jnp.bfloat16), earlier, preferred_element_type=jnp.float32)
    spot = jnp.where(first > 0, rank_first, jnp.where(second > 0, half_rows + rank_second, -1.0))
    place[...] = spot.astype(jnp.int32)
    members[0] = first
    members[1] = second

    blank = jnp.zeros((ROWS, dim_share), jnp.bfloat16)
    packed[n_halves] = blank
    for c in range(chunks):
        for j in range(2):
            cross_in[c][j, capacity] = blank

    row = lax.broadcasted_iota(jnp.int32, (2 * ROWS, length), 0)
    row = jnp.where(row < ROWS, row, row - ROWS + half_rows)
    sum_row = lax.broadcasted_iota(jnp.int32, (ROWS, length), 0)

    def pack_chunk(c):
        def group(g, carry):
            for t in range(GROUP):
                s = g * GROUP + t
                chosen = jnp.where(row + c * ROWS == place[pl.ds(s, 1), :], 1.0, 0.0)
                if c == 0:
                    one = members[0, pl.ds(s, 1), :]
                    two = members[1, pl.ds(s, 1), :]
                    sums = jnp.where(sum_row == 0, one, jnp.where(sum_row == 1, two, 0.0))
                    chosen = jnp.concatenate([chosen, sums], axis=0)
                rows = jnp.dot(
                    chosen.astype(jnp.bfloat16), vec_ref[s], preferred_element_type=jnp.float32
                )
                packed[2 * s] = rows[:ROWS].astype(jnp.bfloat16)
                packed[2 * s + 1] = rows[ROWS : 2 * ROWS].astype(jnp.bfloat16)
                if c == 0:
                    count_one = jnp.sum(one, axis=1, keepdims=True)
                    count_two = jnp.sum(two, axis=1, keepdims=True)
                    cent_ref[pl.ds(2 * s, 1), :] = rows[2 * ROWS : 2 * ROWS + 1] / count_one
                    cent_ref[pl.ds(2 * s + 1, 1), :] = rows[2 * ROWS + 1 : 2 * ROWS + 2] / count_two
            return carry

        lax.fori_loop(0, s_local // GROUP, group, 0)

    def send(src, dst, send_sem, recv_sem, device):
        pltpu.make_async_remote_copy(
            src_ref=src, dst_ref=dst, send_sem=send_sem, recv_sem=recv_sem, device_id=device, device_id_type=MESH
        ).start()

    for c in range(chunks):
        pack_chunk(c)
        if c == 0:
            cent_own[...] = cent_ref[...].astype(jnp.bfloat16)
            pl.semaphore_wait(barrier, peers - 1 + n_rep - 1 + 1)
            send(cent_own, cent_in.at[turn], cent_sem, cent_in_sem.at[turn], post_id(relay))

        def fill_cross(i, carry):
            cross_send[c, i] = packed[cross_ref[i]]
            return carry

        lax.fori_loop(0, capacity, fill_cross, 0, unroll=4)
        send(
            cross_send.at[c],
            cross_in[c].at[turn, pl.ds(0, capacity)],
            cross_sem,
            cross_in_sem.at[c, turn],
            post_id(relay),
        )

        def fill_near(k, carry):
            at = (peer(k) - base) * hslot
            for i in range(hslot):
                near_send[c, k, i] = packed[near_ref[at + i]]
            return carry

        lax.fori_loop(0, peers, fill_near, 0)
        here = pl.ds(c * ROWS, ROWS)
        pltpu.make_async_copy(near_send.at[c, 0], out_ref.at[me, :, here, :], out_sem).start()

        def send_near(k, carry):
            send(near_send.at[c, k], out_ref.at[me, :, here, :], near_sem, out_sem, post_id(peer(k)))
            if c == 0:
                send(cent_own, cent_all.at[me], cent_sem, cent_all_sem, post_id(peer(k)))
            return carry

        lax.fori_loop(1, peers, send_near, 0)
        if c == 0:
            pltpu.make_async_copy(cent_own, cent_all.at[me], cent_all_sem).start()

    @pl.when(is_relay)
    def _():
        for j in range(2):
            wait_bytes(cent_in.at[j], cent_in_sem.at[j])
            origin = first_source + j * lanes
            pltpu.make_async_copy(cent_in.at[j], cent_all.at[origin], cent_all_sem).start()

            def forward_cent(k, carry):
                send(cent_in.at[j], cent_all.at[origin], cent_fwd_sem, cent_all_sem, post_id(peer(k)))
                return carry

            lax.fori_loop(1, peers, forward_cent, 0)

    def share_cents():
        wait_bytes(cent_all, cent_all_sem)
        for k in range(1, n_rep):
            send(cent_all, cent_rep.at[k - 1], rep_sem, rep_in_sem.at[k - 1], rep_id(k))

    def relay_chunk(c):
        for j in range(2):
            wait_bytes(cross_in[c].at[j, pl.ds(0, capacity)], cross_in_sem.at[c, j])
        here = pl.ds(c * ROWS, ROWS)
        for j in range(2):
            origin = first_source + j * lanes

            def fill(k, carry):
                at = (j * peers + peer(k) - base) * hslot
                for i in range(hslot):
                    relay_send[c, j, k, i] = cross_in[c][j, relay_ref[at + i]]
                return carry

            lax.fori_loop(0, peers, fill, 0)
            pltpu.make_async_copy(relay_send.at[c, j, 0], out_ref.at[origin, :, here, :], out_sem).start()

            def forward(k, carry):
                send(
                    relay_send.at[c, j, k],
                    out_ref.at[origin, :, here, :],
                    relay_sem,
                    out_sem,
                    post_id(peer(k)),
                )
                return carry

            lax.fori_loop(1, peers, forward, 0)

    for c in range(chunks):

        @pl.when(is_relay)
        def _():
            relay_chunk(c)

        if c == 1:
            share_cents()

    wait_bytes(cross_send, cross_sem)
    wait_bytes(near_send.at[:, pl.ds(1, peers - 1)], near_sem)
    wait_bytes(cent_all.at[pl.ds(0, peers)], cent_sem)
    wait_bytes(cent_rep, rep_sem)
    for k in range(1, n_rep):
        wait_bytes(cent_rep.at[k - 1], rep_in_sem.at[k - 1])

    @pl.when(is_relay)
    def _():
        wait_bytes(relay_send.at[:, :, pl.ds(1, peers - 1)], relay_sem)
        wait_bytes(cent_all.at[pl.ds(0, 2 * peers - 2)], cent_fwd_sem)

    wait_bytes(out_ref, out_sem)


def exchange(call_id, cross, near, relayed, vectors, labels, lengths, n_post, n_rep, hslot):
    s_local, length, dim_share = vectors.shape
    half_rows = length // 2
    n_halves = 2 * s_local
    capacity = cross.shape[0]
    peers = n_post // 2
    chunks = half_rows // ROWS
    bf16 = jnp.bfloat16
    in_smem = pl.BlockSpec(memory_space=pltpu.SMEM)
    in_vmem = pl.BlockSpec(memory_space=pltpu.VMEM)
    in_any = pl.BlockSpec(memory_space=pl.ANY)
    dma = pltpu.SemaphoreType.DMA
    return pl.pallas_call(
        exchange_kernel,
        in_specs=[in_smem] * 3 + [in_vmem] * 3,
        out_specs=[in_any, in_vmem, in_any, in_any],
        out_shape=[
            jax.ShapeDtypeStruct((n_post, hslot, half_rows, dim_share), bf16),
            jax.ShapeDtypeStruct((n_halves, dim_share), jnp.float32),
            jax.ShapeDtypeStruct((n_post, n_halves, dim_share), bf16),
            jax.ShapeDtypeStruct((n_rep - 1, n_post, n_halves, dim_share), bf16),
        ],
        scratch_shapes=[
            pltpu.VMEM((n_halves + 1, ROWS, dim_share), bf16),
            pltpu.VMEM((s_local, length), jnp.int32),
            pltpu.VMEM((2, s_local, length), jnp.float32),
            pltpu.VMEM((chunks, capacity, ROWS, dim_share), bf16),
            pltpu.VMEM((chunks, peers, hslot, ROWS, dim_share), bf16),
            pltpu.VMEM((chunks, 2, peers, hslot, ROWS, dim_share), bf16),
            pltpu.VMEM((n_halves, dim_share), bf16),
            pltpu.VMEM((2, n_halves, dim_share), bf16),
            dma,
            dma,
            dma,
            dma,
            dma,
            dma,
            dma((2,)),
            dma,
            dma,
            dma((n_rep - 1,)),
            dma((chunks, 2)),
        ]
        + [pltpu.VMEM((2, capacity + 1, ROWS, dim_share), bf16)] * chunks,
        compiler_params=pltpu.CompilerParams(
            collective_id=call_id, has_side_effects=True, vmem_limit_bytes=56 * 2**20
        ),
        cost_estimate=pl.CostEstimate(
            flops=4 * n_halves * half_rows * length * dim_share,
            bytes_accessed=2 * vectors.size + 4 * n_post * hslot * half_rows * dim_share,
            transcendentals=0,
        ),
    )(cross, near, relayed, vectors, labels, lengths[:, None])


def pick(mask, values, missing):
    found = jnp.sum(jnp.where(mask, values + 1, 0), axis=-1)
    return jnp.where(found > 0, found - 1, missing).astype(jnp.int32)


def routes(new_owners, n_post, hslot):
    n_halves = new_owners.size
    peers = n_post // 2
    lanes = n_post // 4
    me = lax.axis_index("post")
    owners = lax.all_gather(new_owners.reshape(1, -1), "post", axis=0, tiled=True)
    order = jnp.arange(n_halves)
    is_before = order[None, None, :] < order[None, :, None]
    same = (owners[:, :, None] == owners[:, None, :]) & is_before
    slot = jnp.sum(same.astype(jnp.int32), axis=2)
    crossing = owners // peers != (jnp.arange(n_post) // peers)[:, None]
    rank = jnp.sum((crossing[:, None, :] & is_before).astype(jnp.int32), axis=2)
    most = jnp.max(jnp.sum(crossing.astype(jnp.int32), axis=1))
    side = me // peers
    target = jnp.where(owners // peers == side, (owners - side * peers) * hslot + slot, -1)
    slots = jnp.arange(peers * hslot)
    sources = (1 - side) * peers + lax.rem(me, lanes) + jnp.arange(2) * lanes
    one = lambda array: lax.dynamic_index_in_dim(array, me, 0, keepdims=False)
    rank_mine = jnp.where(one(crossing), one(rank), -1)
    cross = pick(rank_mine[None, :] == order[:, None], order[None, :], n_halves)
    near = pick(one(target)[None, :] == slots[:, None], order[None, :], n_halves)
    relayed = pick(
        target[sources][:, None, :] == slots[None, :, None], rank[sources][:, None, :], n_halves
    )
    return cross, near, relayed.reshape(-1), most


def body(
    split_vectors,
    split_labels,
    split_lengths,
    new_owners,
    neighbour_ids,
    resident_vectors,
    resident_centroids,
    resident_lengths,
):
    n_post = lax.axis_size("post")
    s_local, length, dim_share = split_vectors.shape
    half_rows = length // 2
    hslot = max(2, 4 * s_local // n_post)
    res_local = resident_vectors.shape[0]
    n_rep = lax.axis_size("rep")
    res_part = res_local // n_rep
    post_index = lax.axis_index("post")
    rep_index = lax.axis_index("rep")
    mine_at = rep_index * res_part

    def shifted(array, offset):
        if offset == 0:
            return array
        return lax.ppermute(array, "rep", [(i, (i + offset) % n_rep) for i in range(n_rep)])

    def part_of(array, offset):
        at = lax.rem(rep_index + offset, n_rep) * res_part
        return lax.dynamic_slice_in_dim(array, at, res_part, 0)

    rows_shares = [shifted(part_of(resident_vectors, k), k) for k in range(n_rep)]
    current_shares = [shifted(part_of(resident_centroids, k), k) for k in range(n_rep)]

    cross, near, relayed, most = routes(new_owners, n_post, hslot)
    n_halves = 2 * s_local

    def with_room(call_id, capacity):
        return lambda: exchange(
            call_id,
            cross[:capacity],
            near,
            jnp.minimum(relayed, capacity),
            split_vectors,
            split_labels,
            split_lengths,
            n_post,
            n_rep,
            hslot,
        )

    usual = 5 * n_halves // 8
    new_postings, centroids, cent_mine, cent_rep = lax.cond(
        most <= usual, with_room(0, usual), with_room(1, n_halves)
    )
    new_centroids = centroids.reshape(s_local, 2, dim_share)
    n_cents = n_post * n_halves
    cent_shares = [cent_mine.reshape(n_cents, dim_share)]
    cent_shares += [cent_rep[k].reshape(n_cents, dim_share) for k in range(n_rep - 1)]
    my_postings = post_index * res_local + mine_at + jnp.arange(res_part)
    hits = jnp.any(neighbour_ids[:, :, None] == my_postings[None, None, :], axis=1)
    hits = jnp.repeat(hits, 2, axis=0).T

    own = 0.0
    row_norm = 0.0
    cent_norm = 0.0
    cross = 0.0
    for rows, current, cents in zip(rows_shares, current_shares, cent_shares):
        wide = rows.astype(jnp.float32)
        gap = wide - current.astype(jnp.float32)[:, None, :]
        own += jnp.sum(gap * gap, axis=2)
        row_norm += jnp.sum(wide * wide, axis=2)
        cents_wide = cents.astype(jnp.float32)
        cent_norm += jnp.sum(cents_wide * cents_wide, axis=1)
        cross += lax.dot_general(
            rows.reshape(res_part * length, dim_share),
            cents,
            (((1,), (1,)), ((), ())),
            preferred_element_type=jnp.float32,
        )
    distance = row_norm[:, :, None] - 2.0 * cross.reshape(res_part, length, n_cents) + cent_norm
    distance = jnp.where(hits[:, None, :], distance, far_value)
    best_dist = jnp.minimum(own, jnp.min(distance, axis=2))
    scores = (best_dist - row_norm) / math.sqrt(n_rep * dim_share)
    lengths_mine = part_of(resident_lengths, 0)
    scores = jnp.where(jnp.arange(length)[None, :] < lengths_mine[:, None], scores, 0.0)
    rescore = lax.all_gather(scores, "rep", axis=0, tiled=True)
    return (new_postings, new_centroids, rescore)


def solution(mesh):
    return jax.shard_map(
        body,
        mesh=mesh,
        in_specs=(
            P("post", None, "rep"),
            P("post", None),
            P("post"),
            P("post", None),
            P(),
            P("post", None, "rep"),
            P("post", "rep"),
            P("post"),
        ),
        out_specs=(P("post", None, None, "rep"), P("post", None, "rep"), P("post", None)),
        check_vma=False,
    )
```

time: 379 us -> 288 us (0.76)
  waiting for transfers between devices: 295 us -> 0.01 us
  Pallas kernels: 24.8 us -> 229 us
  blocking collectives: 3.5 us -> 19.3 us
  between operations: 14.2 us -> 1.52 us
  starting transfers between devices: 8.46 us -> 1.47 us
  local copies, waits for them, and re-layouts: 24.2 us -> 19.6 us
  other arithmetic: 4.77 us -> 8.58 us
    all_to_all x1 -> x0, waiting for transfers between devices: 224 us -> none  [body(): lax.all_to_all(outgoing, 'post', split_axis=0, concat_axis=0, tiled=True)]
    pallas_call x1, Pallas kernels: 24.8 us -> 229 us  [exchange(): pl.pallas_call(exchange_kernel, in_specs=[in_smem] * 3 + [in_vmem] * 3, o...]
    all_gather x1 -> x0, waiting for transfers between devices: 38.4 us -> none  [body(): lax.all_gather(centroids.astype(jnp.bfloat16), 'post', axis=0, tiled=True)]
    ppermute x3 -> x2, waiting for transfers between devices: 32.5 us -> 0.01 us  [shifted(): lax.ppermute(array, 'rep', [(i, (i + offset) % n_rep) for i in range(n_re...]
    all_gather x0 -> x1, blocking collectives: none -> 16.1 us  [routes(): lax.all_gather(new_owners.reshape(1, -1), 'post', axis=0, tiled=True)]
    unnamed x19 -> x10, local copies, waits for them, and re-layouts: 20.5 us -> 12.2 us
    all_to_all x1 -> x0, starting transfers between devices: 6.62 us -> none  [body(): lax.all_to_all(outgoing, 'post', split_axis=0, concat_axis=0, tiled=True)]
  transfers between devices with their start and end apart: 5 -> 2, of which waited for: 4 -> 0; matrix products, arithmetic and copies ran while one was open for 3% -> 5% of each run, Pallas kernels for 0% -> 81%
where the time goes in v2:
time: 288 us; the launch traced here: 285 us
  Pallas kernels  229 us (80%)
  local copies, waits for them, and re-layouts  19.6 us (7%)
  blocking collectives  19.3 us (7%)
  other arithmetic  8.58 us (3%)
  matrix products  4.96 us (2%)
    pallas_call x1, Pallas kernels, exchange(): pl.pallas_call(exchange_kernel, in_specs=[in_smem] * 3 + [in_vmem] * 3, o...  229 us
    all_gather x1, blocking collectives, routes(): lax.all_gather(new_owners.reshape(1, -1), 'post', axis=0, tiled=True)  16.1 us
    unnamed x10, local copies, waits for them, and re-layouts  12.2 us
  transfers between devices with their start and end apart: 2, of which 0 were waited for; matrix products, arithmetic and copies ran while one was open for 5% of the time, Pallas kernels for 81%

profile of v2, /device:TPU:15, one launch (start us, length us, event | category | flops | bytes accessed | tf_op | source)
XLA Modules:
  0.0 284.9 jit_solution(10271028852922587627)
XLA Ops:
  0.6 2.1 constant_dynamic-slice_fusion.2
  2.7 0.2 collective-permute-start
  2.9 1.4 constant_dynamic-slice_fusion.4
  4.3 1.2 collective-permute-start.1
  5.6 0.8 copy.27
  6.4 0.1 reshape.155
  6.5 16.1 %all-gather = s32[16,1,64]{2,1,0:T(1,128)S(1)} all-gather(s32[1,1,64]{2,1,0:T(1,128)S(1)} %reshape.155), channel_id=1, replica_groups=mesh['post'=16,'rep'=2] {'post'}, dimensions={0}, use_global_device_ids=true | all-gather | bytes 4352 | tf_op jit(solution)/shard_map/all_gather | solution.py:329
  22.5 0.2 convert_reduce_fusion.2
  22.7 0.8 convert_reduce_fusion.1
  23.6 0.6 gather_fusion
  24.2 0.6 gather_fusion.1
  24.7 0.1 select_reduce_fusion.1
  24.9 0.1 select_n.97
  24.9 0.1 select_reduce_fusion.2
  25.1 0.6 reduce_max.9
  26.4 231.4 %conditional.1 = ((bf16[16,8,96,512]{3,2,1,0:T(8,128)(2,1)}, f32[64,512]{1,0:T(8,128)S(1)}, bf16[16,64,512]{2,1,0:T(8,128)(2,1)S(1)}, bf16[1,16,64,512]{3,2,1,0:T(8,128)(2,1)S(1)})) conditional(s32[]{:T(128)} %convert_element_type.33, (s32[128]{0:T(128)S(1)}, s32[32]{0:T(128)}, s32[64]{0:T(128)S(1)}, s32[64]{0:T(128)S(1)}, ...), branch_computations={%region_7.8_spmd, %region_8.9_spmd} | conditional | flops 2415919104 | bytes 31458568 | solution.py:402
  26.4 1.3 copy.26.length_ref
  27.7 0.5 broadcast_minimum_fusion.1.relay_ref
  28.3 229.5 %branch_1_fun.1 = (bf16[16,8,96,512]{3,2,1,0:T(8,128)(2,1)}, f32[64,512]{1,0:T(8,128)S(1)}, bf16[16,64,512]{2,1,0:T(8,128)(2,1)S(1)}, bf16[1,16,64,512]{3,2,1,0:T(8,128)(2,1)S(1)}) custom-call(s32[40]{0:T(128)S(1)} %bitcast.34, s32[64]{0:T(128)S(1)} %get-tuple-element.45.near_ref, s32[128]{0:T(128)} %broadcast_minimum_fusion.1.relay_ref, ...), custom_call_target="tpu_custom_call" | custom-call | flops 2415919104 | bytes 31457280 | tf_op jit(solution)/shard_map/cond/branch_1_fun/pallas_call | solution.py:276
  257.8 0.0 copy-start
  257.8 0.0 copy-start.1
  257.8 0.3 multiply_reduce_fusion
  258.1 0.3 multiply_reduce_fusion.1
  258.3 0.0 copy-start.2
  258.4 1.7 fusion.1
  260.1 0.0 copy-done
  260.1 0.0 copy-done.1
  260.1 2.2 fusion.11
  262.4 0.0 copy-done.2
  262.4 0.2 compare_reduce_fusion
  262.5 0.1 add.152
  262.6 0.3 broadcast_in_dim.104
  262.9 0.7 reshape.133
  263.6 0.7 dynamic_slice.29
  264.4 0.7 reshape.160
  265.1 0.0 collective-permute-done.1
  265.1 0.7 convert_element_type.39
  265.8 0.0 collective-permute-done
  265.8 1.6 fusion.4
  267.4 0.1 add.149
  267.4 2.7 select_reduce_fusion
  270.2 0.1 reduce_min.12
  270.2 0.1 select_bitcast_fusion
  270.3 3.2 %all-gather.1 = f32[2,4,192]{2,1,0:T(4,128)S(1)} all-gather(f32[1,4,192]{2,1,0:T(4,128)S(1)} %select_bitcast_fusion), channel_id=1, replica_groups=mesh['post'=16,'rep'=2] {'rep'}, dimensions={0}, use_global_device_ids=true | all-gather | bytes 9216 | tf_op jit(solution)/shard_map/all_gather | solution.py:436
  273.5 0.6 reshape.158
  274.1 10.8 %copy.37 = bf16[16,8,96,512]{3,2,1,0:T(8,128)(2,1)} copy(bf16[16,8,96,512]{3,2,1,0:T(8,128)(2,1)} %get-tuple-element.103) | data formatting | bytes 25165824
  (14 shorter events, 0.1 us)
Async XLA Ops:
  2.7 263.1 %collective-permute-start = (bf16[4,192,512]{2,1,0:T(8,128)(2,1)}, bf16[4,192,512]{2,1,0:T(8,128)(2,1)}, u32[]{:S(2)}, u32[]{:S(2)}) collective-permute-start(bf16[4,192,512]{2,1,0:T(8,128)(2,1)} %constant_dynamic-slice_fusion.2), channel_id=1, source_target_pairs={{0,1},{1,0},{2,3},{3,2},{4,5},{5,4},{6,7},{7,6},{8,9},{9,8},{10,11... | collective-permute-start | bytes 2359304 | tf_op jit(solution)/shard_map/ppermute | solution.py:375
  4.3 260.8 %collective-permute-start.1 = (bf16[4,512]{1,0:T(4,128)(2,1)}, bf16[4,512]{1,0:T(4,128)(2,1)}, u32[]{:S(2)}, u32[]{:S(2)}) collective-permute-start(bf16[4,512]{1,0:T(4,128)(2,1)} %get-tuple-element.86), channel_id=1, source_target_pairs={{0,1},{1,0},{2,3},{3,2},{4,5},{5,4},{6,7},{7,6},{8,9},{9,8},{10,11... | collective-permute-start | bytes 12296 | tf_op jit(solution)/shard_map/ppermute | solution.py:375
  257.8 2.3 copy-start
  257.8 2.3 copy-start.1
  258.3 4.0 %copy-start.2 = (s32[512,64]{0,1:T(8,128)S(1)}, s32[512,64]{0,1:T(8,128)}, u32[]{:S(2)}) copy-start(s32[512,64]{0,1:T(8,128)} %param.14) | copy-start | bytes 393220

commit v3 on v2

--- a/solution.py
+++ b/solution.py
@@ -25,10 +25,20 @@
     vec_ref,
     label_ref,
     length_ref,
+    nb_ref,
+    res_ref,
+    cur_ref,
+    res_length_ref,
     out_ref,
     cent_ref,
+    score_ref,
     cent_all,
     cent_rep,
+    rows_in,
+    cur_in,
+    best,
+    score_own,
+    stage,
     packed,
     place,
     members,
@@ -48,6 +58,12 @@
     rep_sem,
     rep_in_sem,
     cross_in_sem,
+    rows_sem,
+    rows_in_sem,
+    cur_sem,
+    cur_in_sem,
+    score_sem,
+    score_in_sem,
     *cross_in,
 ):
     n_post = lax.axis_size("post")
@@ -70,6 +86,7 @@
     hslot = out_ref.shape[1]
     capacity = cross_send.shape[1]
     chunks = half_rows // ROWS
+    res_part = res_ref.shape[0] // n_rep
 
     def peer(k):
         return base + lax.rem(me - base + k, peers)
@@ -140,8 +157,12 @@
                 if c == 0:
                     count_one = jnp.sum(one, axis=1, keepdims=True)
                     count_two = jnp.sum(two, axis=1, keepdims=True)
-                    cent_ref[pl.ds(2 * s, 1), :] = rows[2 * ROWS : 2 * ROWS + 1] / count_one
-                    cent_ref[pl.ds(2 * s + 1, 1), :] = rows[2 * ROWS + 1 : 2 * ROWS + 2] / count_two
+                    cent_one = rows[2 * ROWS : 2 * ROWS + 1] / count_one
+                    cent_two = rows[2 * ROWS + 1 : 2 * ROWS + 2] / count_two
+                    cent_ref[pl.ds(2 * s, 1), :] = cent_one
+                    cent_ref[pl.ds(2 * s + 1, 1), :] = cent_two
+                    stage[pl.ds(s, 1), :] = cent_one
+                    stage[pl.ds(s_local + s, 1), :] = cent_two
             return carry
 
         lax.fori_loop(0, s_local // GROUP, group, 0)
@@ -154,7 +175,7 @@
     for c in range(chunks):
         pack_chunk(c)
         if c == 0:
-            cent_own[...] = cent_ref[...].astype(jnp.bfloat16)
+            cent_own[...] = stage[...].astype(jnp.bfloat16)
             pl.semaphore_wait(barrier, peers - 1 + n_rep - 1 + 1)
             send(cent_own, cent_in.at[turn], cent_sem, cent_in_sem.at[turn], post_id(relay))
 
@@ -190,6 +211,10 @@
         lax.fori_loop(1, peers, send_near, 0)
         if c == 0:
             pltpu.make_async_copy(cent_own, cent_all.at[me], cent_all_sem).start()
+            for k in range(1, n_rep):
+                theirs = pl.ds(lax.rem(rep + k, n_rep) * res_part, res_part)
+                send(res_ref.at[theirs], rows_in.at[k - 1], rows_sem.at[k - 1], rows_in_sem.at[k - 1], rep_id(k))
+                send(cur_ref, cur_in.at[k - 1], cur_sem.at[k - 1], cur_in_sem.at[k - 1], rep_id(k))
 
     @pl.when(is_relay)
     def _():
@@ -208,6 +233,66 @@
         wait_bytes(cent_all, cent_all_sem)
         for k in range(1, n_rep):
             send(cent_all, cent_rep.at[k - 1], rep_sem, rep_in_sem.at[k - 1], rep_id(k))
+
+    def rescore():
+        for k in range(n_rep - 1):
+            wait_bytes(cent_rep.at[k], rep_in_sem.at[k])
+            wait_bytes(rows_in.at[k], rows_in_sem.at[k])
+            wait_bytes(cur_in.at[k], cur_in_sem.at[k])
+        first_mine = rep * res_part
+        contract = (((1,), (1,)), ((), ()))
+
+        def rows_of(k, q):
+            return res_ref[first_mine + q] if k == 0 else rows_in[k - 1, q]
+
+        def scores(vectors_of, count, q):
+            norm = 0.0
+            cross = 0.0
+            for k in range(n_rep):
+                vectors = vectors_of(k)
+                wide = vectors.astype(jnp.float32)
+                norm += jnp.sum(wide * wide, axis=1, keepdims=True)
+                cross += lax.dot_general(
+                    vectors, rows_of(k, q), contract, preferred_element_type=jnp.float32
+                )
+            return norm - 2.0 * cross
+
+        postings = res_ref.shape[0]
+        which = lax.broadcasted_iota(jnp.int32, (postings, length), 0)
+        for q in range(res_part):
+            own = scores(lambda k: cur_ref[...] if k == 0 else cur_in[k - 1], postings, q)
+            own = jnp.where(which == first_mine + q, own, far_value)
+            best[q : q + 1, :] = jnp.min(own, axis=0, keepdims=True)
+
+        def group(g, carry):
+            def cents_of(k):
+                if k == 0:
+                    block = cent_all[pl.ds(g * GROUP, GROUP)]
+                else:
+                    block = cent_rep[k - 1, pl.ds(g * GROUP, GROUP)]
+                return block.reshape(GROUP * n_halves, dim_share)
+
+            named = nb_ref[pl.ds(g * GROUP * s_local, GROUP * s_local), :]
+            for q in range(res_part):
+                posting = me * postings + first_mine + q
+                hit = jnp.max(jnp.where(named == posting, 1.0, 0.0), axis=1, keepdims=True)
+                hit = hit.reshape(GROUP, 1, s_local, 1)
+                hit = jnp.concatenate([hit, hit], axis=1).reshape(GROUP * n_halves, 1)
+                candidate = scores(cents_of, GROUP * n_halves, q)
+                candidate = jnp.where(hit > 0.5, candidate, far_value)
+                least = jnp.min(candidate, axis=0, keepdims=True)
+                best[q : q + 1, :] = jnp.minimum(best[q : q + 1, :], least)
+            return carry
+
+        lax.fori_loop(0, n_post // GROUP, group, 0)
+        lane_id = lax.broadcasted_iota(jnp.int32, (1, length), 1)
+        for q in range(res_part):
+            inside = lane_id < res_length_ref[first_mine + q]
+            score = best[q : q + 1, :] * (1.0 / math.sqrt(n_rep * dim_share))
+            score_own[q : q + 1, :] = jnp.where(inside, score, 0.0)
+        score_ref[rep] = score_own[...]
+        for k in range(1, n_rep):
+            send(score_own, score_ref.at[rep], score_sem.at[k - 1], score_in_sem.at[k - 1], rep_id(k))
 
     def relay_chunk(c):
         for j in range(2):
@@ -243,15 +328,20 @@
         def _():
             relay_chunk(c)
 
-        if c == 1:
+        if c == chunks // 2 - 1:
             share_cents()
+        if c == chunks // 2:
+            rescore()
 
     wait_bytes(cross_send, cross_sem)
     wait_bytes(near_send.at[:, pl.ds(1, peers - 1)], near_sem)
     wait_bytes(cent_all.at[pl.ds(0, peers)], cent_sem)
     wait_bytes(cent_rep, rep_sem)
-    for k in range(1, n_rep):
-        wait_bytes(cent_rep.at[k - 1], rep_in_sem.at[k - 1])
+    for k in range(n_rep - 1):
+        wait_bytes(rows_in.at[k], rows_sem.at[k])
+        wait_bytes(cur_in.at[k], cur_sem.at[k])
+        wait_bytes(score_own, score_sem.at[k])
+        wait_bytes(score_own, score_in_sem.at[k])
 
     @pl.when(is_relay)
     def _():
@@ -261,11 +351,13 @@
     wait_bytes(out_ref, out_sem)
 
 
-def exchange(call_id, cross, near, relayed, vectors, labels, lengths, n_post, n_rep, hslot):
+def exchange(call_id, cross, near, relayed, vectors, labels, lengths, residents, n_post, n_rep, hslot):
     s_local, length, dim_share = vectors.shape
     half_rows = length // 2
     n_halves = 2 * s_local
     capacity = cross.shape[0]
+    postings = residents[1].shape[0]
+    res_part = postings // n_rep
     peers = n_post // 2
     chunks = half_rows // ROWS
     bf16 = jnp.bfloat16
@@ -275,15 +367,21 @@
     dma = pltpu.SemaphoreType.DMA
     return pl.pallas_call(
         exchange_kernel,
-        in_specs=[in_smem] * 3 + [in_vmem] * 3,
-        out_specs=[in_any, in_vmem, in_any, in_any],
+        in_specs=[in_smem] * 3 + [in_vmem] * 6 + [in_smem],
+        out_specs=[in_any, in_vmem, in_vmem],
         out_shape=[
             jax.ShapeDtypeStruct((n_post, hslot, half_rows, dim_share), bf16),
             jax.ShapeDtypeStruct((n_halves, dim_share), jnp.float32),
-            jax.ShapeDtypeStruct((n_post, n_halves, dim_share), bf16),
-            jax.ShapeDtypeStruct((n_rep - 1, n_post, n_halves, dim_share), bf16),
+            jax.ShapeDtypeStruct((n_rep, res_part, length), jnp.float32),
         ],
         scratch_shapes=[
+            pltpu.VMEM((n_post, n_halves, dim_share), bf16),
+            pltpu.VMEM((n_rep - 1, n_post, n_halves, dim_share), bf16),
+            pltpu.VMEM((n_rep - 1, res_part, length, dim_share), bf16),
+            pltpu.VMEM((n_rep - 1, postings, dim_share), bf16),
+            pltpu.VMEM((postings, length), jnp.float32),
+            pltpu.VMEM((res_part, length), jnp.float32),
+            pltpu.VMEM((n_halves, dim_share), jnp.float32),
             pltpu.VMEM((n_halves + 1, ROWS, dim_share), bf16),
             pltpu.VMEM((s_local, length), jnp.int32),
             pltpu.VMEM((2, s_local, length), jnp.float32),
@@ -304,6 +402,7 @@
             dma((n_rep - 1,)),
             dma((chunks, 2)),
         ]
+        + [dma((n_rep - 1,))] * 6
         + [pltpu.VMEM((2, capacity + 1, ROWS, dim_share), bf16)] * chunks,
         compiler_params=pltpu.CompilerParams(
             collective_id=call_id, has_side_effects=True, vmem_limit_bytes=56 * 2**20
@@ -313,7 +412,7 @@
             bytes_accessed=2 * vectors.size + 4 * n_post * hslot * half_rows * dim_share,
             transcendentals=0,
         ),
-    )(cross, near, relayed, vectors, labels, lengths[:, None])
+    )(cross, near, relayed, vectors, labels, lengths[:, None], *residents)
 
 
 def pick(mask, values, missing):
@@ -362,25 +461,7 @@
     s_local, length, dim_share = split_vectors.shape
     half_rows = length // 2
     hslot = max(2, 4 * s_local // n_post)
-    res_local = resident_vectors.shape[0]
     n_rep = lax.axis_size("rep")
-    res_part = res_local // n_rep
-    post_index = lax.axis_index("post")
-    rep_index = lax.axis_index("rep")
-    mine_at = rep_index * res_part
-
-    def shifted(array, offset):
-        if offset == 0:
-            return array
-        return lax.ppermute(array, "rep", [(i, (i + offset) % n_rep) for i in range(n_rep)])
-
-    def part_of(array, offset):
-        at = lax.rem(rep_index + offset, n_rep) * res_part
-        return lax.dynamic_slice_in_dim(array, at, res_part, 0)
-
-    rows_shares = [shifted(part_of(resident_vectors, k), k) for k in range(n_rep)]
-    current_shares = [shifted(part_of(resident_centroids, k), k) for k in range(n_rep)]
-
     cross, near, relayed, most = routes(new_owners, n_post, hslot)
     n_halves = 2 * s_local
 
@@ -393,47 +474,18 @@
             split_vectors,
             split_labels,
             split_lengths,
+            (neighbour_ids, resident_vectors, resident_centroids, resident_lengths),
             n_post,
             n_rep,
             hslot,
         )
 
     usual = 5 * n_halves // 8
-    new_postings, centroids, cent_mine, cent_rep = lax.cond(
+    new_postings, centroids, scores = lax.cond(
         most <= usual, with_room(0, usual), with_room(1, n_halves)
     )
     new_centroids = centroids.reshape(s_local, 2, dim_share)
-    n_cents = n_post * n_halves
-    cent_shares = [cent_mine.reshape(n_cents, dim_share)]
-    cent_shares += [cent_rep[k].reshape(n_cents, dim_share) for k in range(n_rep - 1)]
-    my_postings = post_index * res_local + mine_at + jnp.arange(res_part)
-    hits = jnp.any(neighbour_ids[:, :, None] == my_postings[None, None, :], axis=1)
-    hits = jnp.repeat(hits, 2, axis=0).T
-
-    own = 0.0
-    row_norm = 0.0
-    cent_norm = 0.0
-    cross = 0.0
-    for rows, current, cents in zip(rows_shares, current_shares, cent_shares):
-        wide = rows.astype(jnp.float32)
-        gap = wide - current.astype(jnp.float32)[:, None, :]
-        own += jnp.sum(gap * gap, axis=2)
-        row_norm += jnp.sum(wide * wide, axis=2)
-        cents_wide = cents.astype(jnp.float32)
-        cent_norm += jnp.sum(cents_wide * cents_wide, axis=1)
-        cross += lax.dot_general(
-            rows.reshape(res_part * length, dim_share),
-            cents,
-            (((1,), (1,)), ((), ())),
-            preferred_element_type=jnp.float32,
-        )
-    distance = row_norm[:, :, None] - 2.0 * cross.reshape(res_part, length, n_cents) + cent_norm
-    distance = jnp.where(hits[:, None, :], distance, far_value)
-    best_dist = jnp.minimum(own, jnp.min(distance, axis=2))
-    scores = (best_dist - row_norm) / math.sqrt(n_rep * dim_share)
-    lengths_mine = part_of(resident_lengths, 0)
-    scores = jnp.where(jnp.arange(length)[None, :] < lengths_mine[:, None], scores, 0.0)
-    rescore = lax.all_gather(scores, "rep", axis=0, tiled=True)
+    rescore = scores.reshape(resident_lengths.shape[0], length)
     return (new_postings, new_centroids, rescore)
 
 

time: 288 us -> 269 us (0.934)
  other arithmetic: 8.58 us -> 2.45 us
  matrix products: 4.96 us -> 0 us
  blocking collectives: 19.3 us -> 15.5 us
    dot_general x2 -> x0, matrix products: 4.96 us -> none  [body(): lax.dot_general(rows.reshape(res_part * length, dim_share), cents, (((1,)...]
    reduce_sum x4 -> x0, other arithmetic: 3.84 us -> none  [the longest x2 3.3 us: body(): own += jnp.sum(gap * gap, axis=2)]
    all_gather x1 -> x0, blocking collectives: 3.18 us -> none  [body(): rescore = lax.all_gather(scores, 'rep', axis=0, tiled=True)]
    unnamed x10 -> x3, local copies, waits for them, and re-layouts: 12.2 us -> 11.6 us
  transfers between devices with their start and end apart: 2 -> 0, of which waited for: 0 -> 0; matrix products, arithmetic and copies ran while one was open for 5% -> 0% of each run, Pallas kernels for 81% -> 0%
where the time goes in v3:
time: 269 us; the launch traced here: 267 us
  Pallas kernels  230 us (86%)
  local copies, waits for them, and re-layouts  17.2 us (6%)
  blocking collectives  15.5 us (6%)
    pallas_call x1, Pallas kernels, exchange(): pl.pallas_call(exchange_kernel, in_specs=[in_smem] * 3 + [in_vmem] * 6 +...  230 us
    all_gather x1, blocking collectives, routes(): lax.all_gather(new_owners.reshape(1, -1), 'post', axis=0, tiled=True)  15.5 us
    unnamed x3, local copies, waits for them, and re-layouts  11.6 us

profile of v3, /device:TPU:15, one launch (start us, length us, event | category | flops | bytes accessed | tf_op | source)
XLA Modules:
  0.0 266.7 jit_solution(1253602758323505757)
XLA Ops:
  0.7 0.8 copy.30
  1.5 0.1 reshape.110
  1.6 15.5 %all-gather = s32[16,1,64]{2,1,0:T(1,128)S(1)} all-gather(s32[1,1,64]{2,1,0:T(1,128)S(1)} %reshape.110), channel_id=1, replica_groups=mesh['post'=16,'rep'=2] {'post'}, dimensions={0}, use_global_device_ids=true | all-gather | bytes 4352 | tf_op jit(solution)/shard_map/all_gather | solution.py:428
  17.1 0.2 convert_reduce_fusion.2
  17.3 0.6 reduce_max.9
  18.6 0.8 convert_reduce_fusion.1
  19.4 0.6 gather_fusion
  20.0 0.6 gather_fusion.1
  20.6 0.1 select_reduce_fusion.1
  20.7 0.1 select_reduce_fusion
  20.8 0.1 select_n.79
  20.9 233.7 %conditional.1 = ((bf16[16,8,96,512]{3,2,1,0:T(8,128)(2,1)}, f32[64,512]{1,0:T(8,128)S(1)}, f32[2,4,192]{2,1,0:T(4,128)S(1)})) conditional(s32[]{:T(128)} %convert_element_type.13, (s32[128]{0:T(128)S(1)}, s32[32]{0:T(128)}, s32[64]{0:T(128)S(1)}, s32[64]{0:T(128)S(1)}, bf16[32,192,512]{2,1,0:T(8,128)(2,1)}, /*index=5*/s32[32,192]{1,0:T(8,128)}, ...), branch_computations={%region_7.8_spmd, %region_8.9_spmd} | conditional | flops 2415919104 | bytes 31720712 | solution.py:484
  20.9 0.5 broadcast_minimum_fusion.1.relay_ref
  21.4 1.3 copy.29.length_ref
  22.8 1.7 copy.32.nb_ref
  24.5 230.1 %branch_1_fun.1 = (bf16[16,8,96,512]{3,2,1,0:T(8,128)(2,1)}, f32[64,512]{1,0:T(8,128)S(1)}, f32[2,4,192]{2,1,0:T(4,128)S(1)}) custom-call(s32[40]{0:T(128)S(1)} %bitcast.15, s32[64]{0:T(128)S(1)} %get-tuple-element.62.near_ref, s32[128]{0:T(128)} %broadcast_minimum_fusion.1.relay_ref, bf16[32,192,512]{2,1,0:T(8,128)(2,1)} %get-tuple-element.64.vec_ref, ...), custom_call_target="tpu_custom_call" | custom-call | flops 2415919104 | bytes 31457280 | tf_op jit(solution)/shard_map/cond/branch_1_fun/pallas_call | solution.py:368
  254.6 0.6 reshape.92
  255.2 0.7 reshape.93
  255.9 10.8 %copy.40 = bf16[16,8,96,512]{3,2,1,0:T(8,128)(2,1)} copy(bf16[16,8,96,512]{3,2,1,0:T(8,128)(2,1)} %get-tuple-element.180) | data formatting | bytes 25165824
  (11 shorter events, 0.1 us)

commit v4 on v3

--- a/solution.py
+++ b/solution.py
@@ -21,17 +21,21 @@
 def exchange_kernel(
     cross_ref,
     near_ref,
-    relay_ref,
+    count_ref,
+    res_length_ref,
+    meta_ref,
     vec_ref,
     label_ref,
     length_ref,
     nb_ref,
     res_ref,
     cur_ref,
-    res_length_ref,
     out_ref,
     cent_ref,
     score_ref,
+    most_ref,
+    meta_in,
+    meta,
     cent_all,
     cent_rep,
     rows_in,
@@ -64,6 +68,9 @@
     cur_in_sem,
     score_sem,
     score_in_sem,
+    meta_sem,
+    meta_in_sem,
+    meta_here_sem,
     *cross_in,
 ):
     n_post = lax.axis_size("post")
@@ -175,15 +182,18 @@
     for c in range(chunks):
         pack_chunk(c)
         if c == 0:
-            cent_own[...] = stage[...].astype(jnp.bfloat16)
+            cent_own[pl.ds(0, n_halves), :] = stage[...].astype(jnp.bfloat16)
+            count = jnp.full((ROWS, dim_share), count_ref[0].astype(jnp.float32), jnp.float32)
+            cent_own[pl.ds(n_halves, ROWS), :] = count.astype(jnp.bfloat16)
             pl.semaphore_wait(barrier, peers - 1 + n_rep - 1 + 1)
+            send(meta_ref, meta_in.at[turn], meta_sem, meta_in_sem.at[turn], post_id(relay))
             send(cent_own, cent_in.at[turn], cent_sem, cent_in_sem.at[turn], post_id(relay))
 
         def fill_cross(i, carry):
             cross_send[c, i] = packed[cross_ref[i]]
             return carry
 
-        lax.fori_loop(0, capacity, fill_cross, 0, unroll=4)
+        lax.fori_loop(0, capacity, fill_cross, 0, unroll=2)
         send(
             cross_send.at[c],
             cross_in[c].at[turn, pl.ds(0, capacity)],
@@ -219,6 +229,11 @@
     @pl.when(is_relay)
     def _():
         for j in range(2):
+            wait_bytes(meta_in.at[j], meta_in_sem.at[j])
+            pltpu.make_async_copy(meta_in.at[j], meta.at[j], meta_here_sem.at[j]).start()
+        for j in range(2):
+            wait_bytes(meta.at[j], meta_here_sem.at[j])
+        for j in range(2):
             wait_bytes(cent_in.at[j], cent_in_sem.at[j])
             origin = first_source + j * lanes
             pltpu.make_async_copy(cent_in.at[j], cent_all.at[origin], cent_all_sem).start()
@@ -231,6 +246,8 @@
 
     def share_cents():
         wait_bytes(cent_all, cent_all_sem)
+        counts = cent_all[:, pl.ds(n_halves, ROWS), pl.ds(0, 128)].astype(jnp.float32)
+        most_ref[...] = jnp.max(counts, axis=0)
         for k in range(1, n_rep):
             send(cent_all, cent_rep.at[k - 1], rep_sem, rep_in_sem.at[k - 1], rep_id(k))
 
@@ -267,9 +284,9 @@
         def group(g, carry):
             def cents_of(k):
                 if k == 0:
-                    block = cent_all[pl.ds(g * GROUP, GROUP)]
+                    block = cent_all[pl.ds(g * GROUP, GROUP), pl.ds(0, n_halves)]
                 else:
-                    block = cent_rep[k - 1, pl.ds(g * GROUP, GROUP)]
+                    block = cent_rep[k - 1, pl.ds(g * GROUP, GROUP), pl.ds(0, n_halves)]
                 return block.reshape(GROUP * n_halves, dim_share)
 
             named = nb_ref[pl.ds(g * GROUP * s_local, GROUP * s_local), :]
@@ -302,9 +319,9 @@
             origin = first_source + j * lanes
 
             def fill(k, carry):
-                at = (j * peers + peer(k) - base) * hslot
+                at = (peer(k) - base) * hslot
                 for i in range(hslot):
-                    relay_send[c, j, k, i] = cross_in[c][j, relay_ref[at + i]]
+                    relay_send[c, j, k, i] = cross_in[c][j, meta[j, 0, at + i]]
                 return carry
 
             lax.fori_loop(0, peers, fill, 0)
@@ -333,6 +350,7 @@
         if c == chunks // 2:
             rescore()
 
+    wait_bytes(meta_ref, meta_sem)
     wait_bytes(cross_send, cross_sem)
     wait_bytes(near_send.at[:, pl.ds(1, peers - 1)], near_sem)
     wait_bytes(cent_all.at[pl.ds(0, peers)], cent_sem)
@@ -351,12 +369,13 @@
     wait_bytes(out_ref, out_sem)
 
 
-def exchange(call_id, cross, near, relayed, vectors, labels, lengths, residents, n_post, n_rep, hslot):
+def exchange(call_id, cross, near, count, meta, vectors, labels, lengths, residents, n_post, n_rep, hslot):
+    neighbour_ids, res_vectors, res_centroids, res_lengths = residents
     s_local, length, dim_share = vectors.shape
     half_rows = length // 2
     n_halves = 2 * s_local
     capacity = cross.shape[0]
-    postings = residents[1].shape[0]
+    postings = res_vectors.shape[0]
     res_part = postings // n_rep
     peers = n_post // 2
     chunks = half_rows // ROWS
@@ -367,16 +386,19 @@
     dma = pltpu.SemaphoreType.DMA
     return pl.pallas_call(
         exchange_kernel,
-        in_specs=[in_smem] * 3 + [in_vmem] * 6 + [in_smem],
-        out_specs=[in_any, in_vmem, in_vmem],
+        in_specs=[in_smem] * 4 + [in_vmem] * 7,
+        out_specs=[in_any, in_vmem, in_vmem, in_vmem],
         out_shape=[
             jax.ShapeDtypeStruct((n_post, hslot, half_rows, dim_share), bf16),
             jax.ShapeDtypeStruct((n_halves, dim_share), jnp.float32),
             jax.ShapeDtypeStruct((n_rep, res_part, length), jnp.float32),
+            jax.ShapeDtypeStruct((ROWS, 128), jnp.float32),
         ],
         scratch_shapes=[
-            pltpu.VMEM((n_post, n_halves, dim_share), bf16),
-            pltpu.VMEM((n_rep - 1, n_post, n_halves, dim_share), bf16),
+            pltpu.VMEM((2,) + meta.shape, jnp.int32),
+            pltpu.SMEM((2,) + meta.shape, jnp.int32),
+            pltpu.VMEM((n_post, n_halves + ROWS, dim_share), bf16),
+            pltpu.VMEM((n_rep - 1, n_post, n_halves + ROWS, dim_share), bf16),
             pltpu.VMEM((n_rep - 1, res_part, length, dim_share), bf16),
             pltpu.VMEM((n_rep - 1, postings, dim_share), bf16),
             pltpu.VMEM((postings, length), jnp.float32),
@@ -388,8 +410,8 @@
             pltpu.VMEM((chunks, capacity, ROWS, dim_share), bf16),
             pltpu.VMEM((chunks, peers, hslot, ROWS, dim_share), bf16),
             pltpu.VMEM((chunks, 2, peers, hslot, ROWS, dim_share), bf16),
-            pltpu.VMEM((n_halves, dim_share), bf16),
-            pltpu.VMEM((2, n_halves, dim_share), bf16),
+            pltpu.VMEM((n_halves + ROWS, dim_share), bf16),
+            pltpu.VMEM((2, n_halves + ROWS, dim_share), bf16),
             dma,
             dma,
             dma,
@@ -403,6 +425,7 @@
             dma((chunks, 2)),
         ]
         + [dma((n_rep - 1,))] * 6
+        + [dma, dma((2,)), dma((2,))]
         + [pltpu.VMEM((2, capacity + 1, ROWS, dim_share), bf16)] * chunks,
         compiler_params=pltpu.CompilerParams(
             collective_id=call_id, has_side_effects=True, vmem_limit_bytes=56 * 2**20
@@ -412,7 +435,45 @@
             bytes_accessed=2 * vectors.size + 4 * n_post * hslot * half_rows * dim_share,
             transcendentals=0,
         ),
-    )(cross, near, relayed, vectors, labels, lengths[:, None], *residents)
+    )(
+        cross,
+        near,
+        count,
+        res_lengths,
+        meta,
+        vectors,
+        labels,
+        lengths[:, None],
+        neighbour_ids,
+        res_vectors,
+        res_centroids,
+    )
+
+
+def move_kernel(src_ref, dst_ref, room, in_sem, out_sem):
+    blocks = src_ref.shape[0]
+    for i in range(blocks):
+        pltpu.make_async_copy(src_ref.at[i], room.at[i], in_sem.at[i]).start()
+    for i in range(blocks):
+        pltpu.make_async_copy(src_ref.at[i], room.at[i], in_sem.at[i]).wait()
+        pltpu.make_async_copy(room.at[i], dst_ref.at[i], out_sem.at[i]).start()
+    for i in range(blocks):
+        pltpu.make_async_copy(room.at[i], dst_ref.at[i], out_sem.at[i]).wait()
+
+
+def move(array):
+    return pl.pallas_call(
+        move_kernel,
+        in_specs=[pl.BlockSpec(memory_space=pl.ANY)],
+        out_specs=pl.BlockSpec(memory_space=pl.ANY),
+        out_shape=jax.ShapeDtypeStruct(array.shape, array.dtype),
+        scratch_shapes=[
+            pltpu.VMEM(array.shape, array.dtype),
+            pltpu.SemaphoreType.DMA((array.shape[0],)),
+            pltpu.SemaphoreType.DMA((array.shape[0],)),
+        ],
+        compiler_params=pltpu.CompilerParams(vmem_limit_bytes=40 * 2**20),
+    )(array)
 
 
 def pick(mask, values, missing):
@@ -423,28 +484,20 @@
 def routes(new_owners, n_post, hslot):
     n_halves = new_owners.size
     peers = n_post // 2
-    lanes = n_post // 4
-    me = lax.axis_index("post")
-    owners = lax.all_gather(new_owners.reshape(1, -1), "post", axis=0, tiled=True)
+    side = lax.axis_index("post") // peers
+    owner = new_owners.reshape(-1)
     order = jnp.arange(n_halves)
-    is_before = order[None, None, :] < order[None, :, None]
-    same = (owners[:, :, None] == owners[:, None, :]) & is_before
-    slot = jnp.sum(same.astype(jnp.int32), axis=2)
-    crossing = owners // peers != (jnp.arange(n_post) // peers)[:, None]
-    rank = jnp.sum((crossing[:, None, :] & is_before).astype(jnp.int32), axis=2)
-    most = jnp.max(jnp.sum(crossing.astype(jnp.int32), axis=1))
-    side = me // peers
-    target = jnp.where(owners // peers == side, (owners - side * peers) * hslot + slot, -1)
+    is_before = order[None, :] < order[:, None]
+    slot = jnp.sum(((owner[:, None] == owner[None, :]) & is_before).astype(jnp.int32), axis=1)
+    crossing = owner // peers != side
+    rank = jnp.sum((crossing[None, :] & is_before).astype(jnp.int32), axis=1)
+    target = owner * hslot + slot
     slots = jnp.arange(peers * hslot)
-    sources = (1 - side) * peers + lax.rem(me, lanes) + jnp.arange(2) * lanes
-    one = lambda array: lax.dynamic_index_in_dim(array, me, 0, keepdims=False)
-    rank_mine = jnp.where(one(crossing), one(rank), -1)
-    cross = pick(rank_mine[None, :] == order[:, None], order[None, :], n_halves)
-    near = pick(one(target)[None, :] == slots[:, None], order[None, :], n_halves)
-    relayed = pick(
-        target[sources][:, None, :] == slots[None, :, None], rank[sources][:, None, :], n_halves
-    )
-    return cross, near, relayed.reshape(-1), most
+    cross = pick(jnp.where(crossing, rank, -1)[None, :] == order[:, None], order[None, :], n_halves)
+    near = pick(target[None, :] == side * peers * hslot + slots[:, None], order[None, :], n_halves)
+    meta = pick(target[None, :] == (1 - side) * peers * hslot + slots[:, None], rank[None, :], n_halves)
+    count = jnp.sum(crossing.astype(jnp.int32)).reshape(1)
+    return cross, near, meta, count
 
 
 def body(
@@ -462,15 +515,18 @@
     half_rows = length // 2
     hslot = max(2, 4 * s_local // n_post)
     n_rep = lax.axis_size("rep")
-    cross, near, relayed, most = routes(new_owners, n_post, hslot)
+    cross, near, meta, count = routes(new_owners, n_post, hslot)
     n_halves = 2 * s_local
 
     def with_room(call_id, capacity):
-        return lambda: exchange(
+        table = jnp.minimum(meta, capacity)
+        table = jnp.broadcast_to(jnp.pad(table, (0, -table.size % 128))[None, :], (8, table.size + -table.size % 128))
+        return exchange(
             call_id,
             cross[:capacity],
             near,
-            jnp.minimum(relayed, capacity),
+            count,
+            table,
             split_vectors,
             split_labels,
             split_lengths,
@@ -480,10 +536,14 @@
             hslot,
         )
 
-    usual = 5 * n_halves // 8
-    new_postings, centroids, scores = lax.cond(
-        most <= usual, with_room(0, usual), with_room(1, n_halves)
+    usual = 23 * n_halves // 32
+    stored, centroids, scores, most = with_room(0, usual)
+    stored, _ = lax.while_loop(
+        lambda state: state[1] > usual,
+        lambda state: (with_room(1, n_halves)[0], jnp.float32(0)),
+        (stored, most[0, 0]),
     )
+    new_postings = move(stored)
     new_centroids = centroids.reshape(s_local, 2, dim_share)
     rescore = scores.reshape(resident_lengths.shape[0], length)
     return (new_postings, new_centroids, rescore)

time: 269 us -> 264 us (0.981); the launches traced: 267 us -> 259 us
  Pallas kernels: 230 us -> 249 us
  blocking collectives: 15.5 us -> 0 us
  local copies, waits for them, and re-layouts: 17.2 us -> 6.42 us
    pallas_call x1 -> x2, Pallas kernels: 230 us -> 249 us  [the longest x1 240 us: exchange(): pl.pallas_call(exchange_kernel, in_specs=[in_smem] * 4 + [in_vmem] * 7, o...]
    all_gather x1 -> x0, blocking collectives: 15.5 us -> none  [routes(): lax.all_gather(new_owners.reshape(1, -1), 'post', axis=0, tiled=True)]
    unnamed x3 -> x6, local copies, waits for them, and re-layouts: 11.6 us -> 1.79 us
where the time goes in v4:
time: 264 us; the launch traced here: 259 us
  Pallas kernels  249 us (94%)
  local copies, waits for them, and re-layouts  6.42 us (2%)
    pallas_call x1, Pallas kernels, exchange(): pl.pallas_call(exchange_kernel, in_specs=[in_smem] * 4 + [in_vmem] * 7, o...  240 us
    pallas_call x1, Pallas kernels, move(): pl.pallas_call(move_kernel, in_specs=[pl.BlockSpec(memory_space=pl.ANY)],...  9.07 us

profile of v4, /device:TPU:15, one launch (start us, length us, event | category | flops | bytes accessed | tf_op | source)
XLA Modules:
  0.0 258.8 jit_solution(9343491908105277931)
XLA Ops:
  0.6 1.3 fusion.2
  2.0 1.3 copy.23.length_ref
  3.3 0.8 copy.22
  4.1 0.1 reshape.90
  4.2 0.2 convert_reduce_fusion
  4.4 0.1 convert_reduce_fusion.1
  4.5 0.2 select_reduce_fusion
  4.8 0.6 broadcast_in_dim.65.meta_ref
  5.4 1.0 copy.24.nb_ref
  6.4 240.1 %shard_map.103 = (bf16[16,8,96,512]{3,2,1,0:T(8,128)(2,1)}, f32[64,512]{1,0:T(8,128)}, f32[2,4,192]{2,1,0:T(4,128)}, f32[16,128]{1,0:T(8,128)}) custom-call(s32[46]{0:T(128)S(1)} %bitcast.7, s32[64]{0:T(128)S(1)} %get-tuple-element.169.near_ref, s32[1]{0:T(128)} %bitcast.1.count_ref, s32[8]{0:T(128)} %res_length_ref.1, s32[8,128]{1,0:T(8,128)} %broadcast_in_dim.65.meta_ref, ...), custom_call_target="tpu_custom_call" | custom-call | flops 2415919104 | bytes 31457280 | tf_op jit(solution)/shard_map/pallas_call | solution.py:387
  246.5 1.3 slice.7
  247.7 0.6 while.9
  248.4 0.0 copy-start.1
  248.4 0.0 copy-start
  248.4 9.1 %shard_map.104 = bf16[16,8,96,512]{3,2,1,0:T(8,128)(2,1)} custom-call(bf16[16,8,96,512]{3,2,1,0:T(8,128)(2,1)} %get-tuple-element.75.src_ref), custom_call_target="tpu_custom_call" | custom-call | tf_op jit(solution)/shard_map/pallas_call | solution.py:465
  257.5 0.0 copy-done.1
  257.5 0.6 reshape.93
  258.1 0.0 copy-done
  258.1 0.7 reshape.92
  (9 shorter events, 0.1 us)
Async XLA Ops:
  248.4 9.1 %copy-start.1 = (f32[2,4,192]{2,1,0:T(4,128)S(1)}, f32[2,4,192]{2,1,0:T(4,128)}, u32[]{:S(2)}) copy-start(f32[2,4,192]{2,1,0:T(4,128)} %get-tuple-element.77) | copy-start | bytes 18436
  248.4 9.7 %copy-start = (f32[64,512]{1,0:T(8,128)S(1)}, f32[64,512]{1,0:T(8,128)}, u32[]{:S(2)}) copy-start(f32[64,512]{1,0:T(8,128)} %get-tuple-element.76) | copy-start | bytes 393220

commit v5 on v4

--- a/solution.py
+++ b/solution.py
@@ -10,6 +10,7 @@
 
 far_value = 1e30
 ROWS = 16
+SPANS = 2
 GROUP = 4
 MESH = pl.DeviceIdType.MESH
 
@@ -94,6 +95,7 @@
     capacity = cross_send.shape[1]
     chunks = half_rows // ROWS
     res_part = res_ref.shape[0] // n_rep
+    width = dim_share // SPANS
 
     def peer(k):
         return base + lax.rem(me - base + k, peers)
@@ -138,9 +140,9 @@
 
     blank = jnp.zeros((ROWS, dim_share), jnp.bfloat16)
     packed[n_halves] = blank
-    for c in range(chunks):
-        for j in range(2):
-            cross_in[c][j, capacity] = blank
+    for u in range(chunks * SPANS):
+        for j in range(2):
+            cross_in[u][j, capacity] = blank[:, :width]
 
     row = lax.broadcasted_iota(jnp.int32, (2 * ROWS, length), 0)
     row = jnp.where(row < ROWS, row, row - ROWS + half_rows)
@@ -190,17 +192,20 @@
             send(cent_own, cent_in.at[turn], cent_sem, cent_in_sem.at[turn], post_id(relay))
 
         def fill_cross(i, carry):
-            cross_send[c, i] = packed[cross_ref[i]]
+            rows = packed[cross_ref[i]]
+            for b in range(SPANS):
+                cross_send[c * SPANS + b, i] = rows[:, b * width : (b + 1) * width]
             return carry
 
-        lax.fori_loop(0, capacity, fill_cross, 0, unroll=2)
-        send(
-            cross_send.at[c],
-            cross_in[c].at[turn, pl.ds(0, capacity)],
-            cross_sem,
-            cross_in_sem.at[c, turn],
-            post_id(relay),
-        )
+        lax.fori_loop(0, capacity, fill_cross, 0)
+        for u in range(c * SPANS, (c + 1) * SPANS):
+            send(
+                cross_send.at[u],
+                cross_in[u].at[turn, pl.ds(0, capacity)],
+                cross_sem,
+                cross_in_sem.at[u, turn],
+                post_id(relay),
+            )
 
         def fill_near(k, carry):
             at = (peer(k) - base) * hslot
@@ -311,26 +316,27 @@
         for k in range(1, n_rep):
             send(score_own, score_ref.at[rep], score_sem.at[k - 1], score_in_sem.at[k - 1], rep_id(k))
 
-    def relay_chunk(c):
-        for j in range(2):
-            wait_bytes(cross_in[c].at[j, pl.ds(0, capacity)], cross_in_sem.at[c, j])
-        here = pl.ds(c * ROWS, ROWS)
+    def relay_chunk(u):
+        for j in range(2):
+            wait_bytes(cross_in[u].at[j, pl.ds(0, capacity)], cross_in_sem.at[u, j])
+        here = pl.ds(u // SPANS * ROWS, ROWS)
+        cols = pl.ds(u % SPANS * width, width)
         for j in range(2):
             origin = first_source + j * lanes
 
             def fill(k, carry):
                 at = (peer(k) - base) * hslot
                 for i in range(hslot):
-                    relay_send[c, j, k, i] = cross_in[c][j, meta[j, 0, at + i]]
+                    relay_send[u, j, k, i] = cross_in[u][j, meta[j, 0, at + i]]
                 return carry
 
             lax.fori_loop(0, peers, fill, 0)
-            pltpu.make_async_copy(relay_send.at[c, j, 0], out_ref.at[origin, :, here, :], out_sem).start()
+            pltpu.make_async_copy(relay_send.at[u, j, 0], out_ref.at[origin, :, here, cols], out_sem).start()
 
             def forward(k, carry):
                 send(
-                    relay_send.at[c, j, k],
-                    out_ref.at[origin, :, here, :],
+                    relay_send.at[u, j, k],
+                    out_ref.at[origin, :, here, cols],
                     relay_sem,
                     out_sem,
                     post_id(peer(k)),
@@ -343,7 +349,8 @@
 
         @pl.when(is_relay)
         def _():
-            relay_chunk(c)
+            for u in range(c * SPANS, (c + 1) * SPANS):
+                relay_chunk(u)
 
         if c == chunks // 2 - 1:
             share_cents()
@@ -407,9 +414,9 @@
             pltpu.VMEM((n_halves + 1, ROWS, dim_share), bf16),
             pltpu.VMEM((s_local, length), jnp.int32),
             pltpu.VMEM((2, s_local, length), jnp.float32),
-            pltpu.VMEM((chunks, capacity, ROWS, dim_share), bf16),
+            pltpu.VMEM((chunks * SPANS, capacity, ROWS, dim_share // SPANS), bf16),
             pltpu.VMEM((chunks, peers, hslot, ROWS, dim_share), bf16),
-            pltpu.VMEM((chunks, 2, peers, hslot, ROWS, dim_share), bf16),
+            pltpu.VMEM((chunks * SPANS, 2, peers, hslot, ROWS, dim_share // SPANS), bf16),
             pltpu.VMEM((n_halves + ROWS, dim_share), bf16),
             pltpu.VMEM((2, n_halves + ROWS, dim_share), bf16),
             dma,
@@ -422,11 +429,11 @@
             dma,
             dma,
             dma((n_rep - 1,)),
-            dma((chunks, 2)),
+            dma((chunks * SPANS, 2)),
         ]
         + [dma((n_rep - 1,))] * 6
         + [dma, dma((2,)), dma((2,))]
-        + [pltpu.VMEM((2, capacity + 1, ROWS, dim_share), bf16)] * chunks,
+        + [pltpu.VMEM((2, capacity + 1, ROWS, dim_share // SPANS), bf16)] * (chunks * SPANS),
         compiler_params=pltpu.CompilerParams(
             collective_id=call_id, has_side_effects=True, vmem_limit_bytes=56 * 2**20
         ),
@@ -536,7 +543,7 @@
             hslot,
         )
 
-    usual = 23 * n_halves // 32
+    usual = 45 * n_halves // 64
     stored, centroids, scores, most = with_room(0, usual)
     stored, _ = lax.while_loop(
         lambda state: state[1] > usual,

time: 264 us -> 253 us (0.958)
  Pallas kernels: 249 us -> 240 us
    pallas_call x1, Pallas kernels: 240 us -> 231 us  [exchange(): pl.pallas_call(exchange_kernel, in_specs=[in_smem] * 4 + [in_vmem] * 7, o...]
where the time goes in v5:
time: 253 us; the launch traced here: 250 us
  Pallas kernels  240 us (95%)
  local copies, waits for them, and re-layouts  6.42 us (3%)
    pallas_call x1, Pallas kernels, exchange(): pl.pallas_call(exchange_kernel, in_specs=[in_smem] * 4 + [in_vmem] * 7, o...  231 us
    pallas_call x1, Pallas kernels, move(): pl.pallas_call(move_kernel, in_specs=[pl.BlockSpec(memory_space=pl.ANY)],...  9.07 us

profile of v5, /device:TPU:15, one launch (start us, length us, event | category | flops | bytes accessed | tf_op | source)
XLA Modules:
  0.0 250.0 jit_solution(14274313697736873303)
XLA Ops:
  0.6 1.3 fusion.2
  2.0 1.3 copy.23.length_ref
  3.3 0.8 copy.22
  4.1 0.1 reshape.90
  4.2 0.2 convert_reduce_fusion
  4.4 0.1 convert_reduce_fusion.1
  4.5 0.2 select_reduce_fusion
  4.8 0.6 broadcast_in_dim.65.meta_ref
  5.4 1.0 copy.24.nb_ref
  6.4 231.2 %shard_map.103 = (bf16[16,8,96,512]{3,2,1,0:T(8,128)(2,1)}, f32[64,512]{1,0:T(8,128)}, f32[2,4,192]{2,1,0:T(4,128)}, f32[16,128]{1,0:T(8,128)}) custom-call(s32[45]{0:T(128)S(1)} %bitcast.7, s32[64]{0:T(128)S(1)} %get-tuple-element.169.near_ref, s32[1]{0:T(128)} %bitcast.1.count_ref, s32[8]{0:T(128)} %res_length_ref.1, s32[8,128]{1,0:T(8,128)} %broadcast_in_dim.65.meta_ref, ...), custom_call_target="tpu_custom_call" | custom-call | flops 2415919104 | bytes 31457280 | tf_op jit(solution)/shard_map/pallas_call | solution.py:394
  237.6 1.3 slice.7
  238.9 0.6 while.9
  239.5 0.0 copy-start.1
  239.5 0.0 copy-start
  239.5 9.1 %shard_map.104 = bf16[16,8,96,512]{3,2,1,0:T(8,128)(2,1)} custom-call(bf16[16,8,96,512]{3,2,1,0:T(8,128)(2,1)} %get-tuple-element.75.src_ref), custom_call_target="tpu_custom_call" | custom-call | tf_op jit(solution)/shard_map/pallas_call | solution.py:472
  248.6 0.0 copy-done.1
  248.6 0.6 reshape.93
  249.2 0.0 copy-done
  249.2 0.7 reshape.92
  (9 shorter events, 0.1 us)
Async XLA Ops:
  239.5 9.1 %copy-start.1 = (f32[2,4,192]{2,1,0:T(4,128)S(1)}, f32[2,4,192]{2,1,0:T(4,128)}, u32[]{:S(2)}) copy-start(f32[2,4,192]{2,1,0:T(4,128)} %get-tuple-element.77) | copy-start | bytes 18436
  239.5 9.7 %copy-start = (f32[64,512]{1,0:T(8,128)S(1)}, f32[64,512]{1,0:T(8,128)}, u32[]{:S(2)}) copy-start(f32[64,512]{1,0:T(8,128)} %get-tuple-element.76) | copy-start | bytes 393220
